TPU v7x, 128 devices: a whole 4x4x4 slice. The times are simulated.
128 devices in a mesh: dp: 16 (over y, x_lo, core), seq: 8 (over x_hi, z).
Axes of the slice: x: 4 (x_hi: 2, x_lo: 2; x = x_hi * 2 + x_lo), y: 4, z: 4, core: 2. Of those that a mesh axis runs over, the one named last changes fastest.
Arguments:
- tokens: bfloat16 [16384, 1280], P(('dp', 'seq')), may hold values from -24 to 24
- teacher: bfloat16 [16384, 1280], P(('dp', 'seq')), may hold values from -20 to 20
- prefix: int32 [16], replicated, may hold values from 1 to 1024
- routes: int32 [16384, 2], P(('dp', 'seq')), may hold values from 0 to 2, all different within a row
- attn_gain: bfloat16 [1280], P(('dp', 'seq')), may hold values from 0.099609375 to 1.8984375
- w_qkv: bfloat16 [1280, 3840], P(('dp', 'seq')), may hold values from -0.15625 to 0.15625
- w_out: bfloat16 [1280, 1280], P(('dp', 'seq')), may hold values from -2 to 2
- router_w: bfloat16 [1280, 3], P(('dp', 'seq')), may hold values from -0.078125 to 0.078125
- ffn_gain: bfloat16 [1280], P(('dp', 'seq')), may hold values from 0.099609375 to 1.8984375
- w_gate_up: bfloat16 [1280, 4, 2, 896], P('dp', None, None, 'seq'), may hold values from -0.15625 to 0.15625
- w_down: bfloat16 [1280, 4, 896], P('dp', None, 'seq'), may hold values from -0.1875 to 0.1875
Outputs:
- activations: bfloat16 [16384, 1280], P(('dp', 'seq'))
- loss: float32 [], replicated
- d_tokens: float32 [16384, 1280], P(('dp', 'seq'))
- d_attn_gain: float32 [1280], P(('dp', 'seq'))
- d_w_qkv: float32 [1280, 3840], P(('dp', 'seq'))
- d_w_out: float32 [1280, 1280], P(('dp', 'seq'))
- d_router_w: float32 [1280, 3], P(('dp', 'seq'))
- d_ffn_gain: float32 [1280], P(('dp', 'seq'))
- d_w_gate_up: float32 [1280, 4, 2, 896], P('dp', None, None, 'seq')
- d_w_down: float32 [1280, 4, 896], P('dp', None, 'seq')
Inputs may be any that keep to these rules, and one draw needn't show every extreme that they name: `routes`: each token's 2 routed experts are different.
All inputs are finite; a program needn't handle non-finite values.
Results may differ from a plain program's by a relative error of at most 0.017.
Values may be sent and summed in bfloat16 or wider, within the bound.
No kernel may reach another device: no remote copies, remote signals or barrier semaphores. Data moves between devices by JAX's collectives and lax.ppermute only.
A program may use at most 192 MiB of HBM per device.

v0:
```python
import jax
import jax.numpy as jnp
from jax import lax
from jax.sharding import PartitionSpec as P

HEAD_DIM = 128


norm_eps = 1e-06
masked_score = -1e30
rope_base = 10000.0


def rope_tables(first, count, head_dim):
    places = (first + jnp.arange(count, dtype=jnp.int32)).astype(jnp.float32)
    half_dim = head_dim // 2
    speeds = rope_base ** (-jnp.arange(half_dim, dtype=jnp.float32) / half_dim)
    angles = places[:, None] * speeds[None, :]
    cosine = jnp.concatenate([jnp.cos(angles), jnp.cos(angles)], axis=-1)[:, None, :]
    sine = jnp.concatenate([jnp.sin(angles), jnp.sin(angles)], axis=-1)[:, None, :]
    return (cosine, sine)


def turned(values):
    half_dim = values.shape[-1] // 2
    return jnp.concatenate([-values[..., half_dim:], values[..., :half_dim]], axis=-1)


def inverse_norm(values):
    return lax.rsqrt(jnp.mean(values * values, axis=-1, keepdims=True) + norm_eps)


def norm_back(grad_normed, normed, inverse):
    return inverse * (grad_normed - normed * jnp.mean(grad_normed * normed, axis=-1, keepdims=True))


def combine_of(second_h, router_all, route_rows, routed):
    gates = jax.nn.softmax(
        jnp.dot(second_h, router_all, preferred_element_type=jnp.float32), axis=-1
    )
    chosen = jnp.any(
        route_rows[:, :, None] == jnp.arange(routed, dtype=jnp.int32)[None, None, :], axis=1
    )
    combine = jnp.concatenate(
        [jnp.ones((second_h.shape[0], 1), jnp.float32), jnp.where(chosen, gates, 0.0)], axis=1
    )
    return (gates, chosen, combine)


def on_device(
    tokens, teacher, prefix, routes, attn_gain, w_qkv, w_out, router_w, ffn_gain, w_gate_up, w_down
):
    local_rows, width = tokens.shape
    head_dim = HEAD_DIM
    head_count = width // head_dim
    routed = router_w.shape[1]
    score_scale = head_dim ** (-0.5)
    seq_groups = lax.axis_size("seq")
    seq_place = lax.axis_index("seq")
    seq_length = local_rows * seq_groups
    inputs = tokens.astype(jnp.float32)
    inverse_one = inverse_norm(inputs)
    normed_one = inputs * inverse_one
    attn_gain_all, qkv_all, out_all, ffn_gain_all, router_all = (
        lax.all_gather(attn_gain, ("dp", "seq"), axis=0, tiled=True),
        lax.all_gather(w_qkv, ("dp", "seq"), axis=0, tiled=True),
        lax.all_gather(w_out, ("dp", "seq"), axis=0, tiled=True),
        lax.all_gather(ffn_gain, ("dp", "seq"), axis=0, tiled=True),
        lax.all_gather(router_w, ("dp", "seq"), axis=0, tiled=True),
    )
    first_h = (normed_one * attn_gain_all.astype(jnp.float32)).astype(jnp.bfloat16)
    qkv = jnp.dot(first_h, qkv_all, preferred_element_type=jnp.float32)
    cosine, sine = rope_tables(seq_place * local_rows, local_rows, head_dim)
    query_raw = qkv[:, :width].reshape(local_rows, head_count, head_dim)
    key_raw = qkv[:, width : 2 * width].reshape(local_rows, head_count, head_dim)
    queries = (query_raw * cosine + turned(query_raw) * sine).astype(jnp.bfloat16)
    key_own = (
        (key_raw * cosine + turned(key_raw) * sine).astype(jnp.bfloat16).reshape(local_rows, width)
    )
    value_own = qkv[:, 2 * width :].astype(jnp.bfloat16)
    key_all, value_all = (
        lax.all_gather(key_own, "seq", axis=0, tiled=True),
        lax.all_gather(value_own, "seq", axis=0, tiled=True),
    )
    key_heads = key_all.reshape(seq_length, head_count, head_dim)
    value_heads = value_all.reshape(seq_length, head_count, head_dim)
    prefix_len = prefix[lax.axis_index("dp")]
    query_places = seq_place * local_rows + jnp.arange(local_rows, dtype=jnp.int32)
    key_places = jnp.arange(seq_length, dtype=jnp.int32)
    visible = (key_places[None, :] <= query_places[:, None]) | (key_places[None, :] < prefix_len)

    def attention_scores():
        raw = (
            jnp.einsum("thd,shd->hts", queries, key_heads, preferred_element_type=jnp.float32)
            * score_scale
        )
        return jnp.where(visible[None], raw, masked_score)

    scores = attention_scores()
    top_score = jnp.max(scores, axis=-1, keepdims=True)
    expd = jnp.exp(scores - top_score)
    totals = jnp.sum(expd, axis=-1, keepdims=True)
    probs_low = (expd / totals).astype(jnp.bfloat16)
    log_total = top_score + jnp.log(totals)
    mixed = jnp.einsum("hts,shd->thd", probs_low, value_heads, preferred_element_type=jnp.float32)
    mixed_low = mixed.reshape(local_rows, width).astype(jnp.bfloat16)
    attn = jnp.einsum("ti,oi->to", mixed_low, out_all, preferred_element_type=jnp.float32)
    after_attn = inputs + attn
    inverse_two = inverse_norm(after_attn)
    normed_two = after_attn * inverse_two
    second_h = (normed_two * ffn_gain_all.astype(jnp.float32)).astype(jnp.bfloat16)
    gates, chosen, combine = combine_of(second_h, router_all, routes, routed)
    gate_up_part, down_part = (
        lax.all_gather(w_gate_up, "seq", axis=3, tiled=True),
        lax.all_gather(w_down, "seq", axis=2, tiled=True),
    )
    gate_up_w, down_w = (
        lax.all_gather(gate_up_part, "dp", axis=0, tiled=True),
        lax.all_gather(down_part, "dp", axis=0, tiled=True),
    )
    gate_up = jnp.einsum("td,degf->tegf", second_h, gate_up_w, preferred_element_type=jnp.float32)
    gate_part = gate_up[:, :, 0, :]
    up_part = gate_up[:, :, 1, :]
    sigmoid_gate = jax.nn.sigmoid(gate_part)
    silu_gate = gate_part * sigmoid_gate
    activated = silu_gate * up_part
    hidden = (combine[:, :, None] * activated).astype(jnp.bfloat16)
    expert_part = jnp.einsum("tef,def->td", hidden, down_w, preferred_element_type=jnp.float32)
    outputs = after_attn + expert_part
    diff = outputs - teacher.astype(jnp.float32)
    squares = lax.psum(jnp.sum(diff * diff), ("dp", "seq"))
    loss = squares / (local_rows * lax.axis_size("dp") * seq_groups)
    diff_low = diff.astype(jnp.bfloat16)
    grad_down = jnp.einsum("tef,td->def", hidden, diff_low, preferred_element_type=jnp.float32)
    grad_hidden = jnp.einsum("td,def->tef", diff_low, down_w, preferred_element_type=jnp.float32)
    grad_act = grad_hidden * combine[:, :, None]
    grad_comb_part = jnp.sum(grad_hidden * activated, axis=-1)
    grad_gate = grad_act * up_part * sigmoid_gate * (1.0 + gate_part * (1.0 - sigmoid_gate))
    grad_up = grad_act * silu_gate
    grad_gate_up = jnp.stack([grad_gate, grad_up], axis=2).astype(jnp.bfloat16)
    grad_w_gate_up = jnp.einsum(
        "td,tegf->degf", second_h, grad_gate_up, preferred_element_type=jnp.float32
    )
    grad_second_part = jnp.einsum(
        "tegf,degf->td", grad_gate_up, gate_up_w, preferred_element_type=jnp.float32
    )
    grad_second_exp, grad_combine = (grad_second_part, grad_comb_part)
    grad_gu_rows, grad_down_rows = (
        lax.psum_scatter(
            grad_w_gate_up.astype(jnp.bfloat16), "dp", scatter_dimension=0, tiled=True
        ).astype(jnp.float32),
        lax.psum_scatter(
            grad_down.astype(jnp.bfloat16), "dp", scatter_dimension=0, tiled=True
        ).astype(jnp.float32),
    )
    grad_gate_up_own, grad_down_own = (
        lax.psum_scatter(
            grad_gu_rows.astype(jnp.bfloat16), "seq", scatter_dimension=3, tiled=True
        ).astype(jnp.float32),
        lax.psum_scatter(
            grad_down_rows.astype(jnp.bfloat16), "seq", scatter_dimension=2, tiled=True
        ).astype(jnp.float32),
    )
    grad_pick = jnp.where(chosen, grad_combine[:, 1:], 0.0)
    grad_logits = (gates * (grad_pick - jnp.sum(grad_pick * gates, axis=-1, keepdims=True))).astype(
        jnp.bfloat16
    )
    grad_router = jnp.einsum("td,te->de", second_h, grad_logits, preferred_element_type=jnp.float32)
    grad_second = grad_second_exp + jnp.einsum(
        "te,de->td", grad_logits, router_all, preferred_element_type=jnp.float32
    )
    grad_ffn_gain = jnp.sum(grad_second * normed_two, axis=0)
    grad_after = diff + norm_back(
        grad_second * ffn_gain_all.astype(jnp.float32), normed_two, inverse_two
    )
    grad_attn_low = grad_after.astype(jnp.bfloat16)
    grad_out = jnp.einsum("to,ti->oi", grad_attn_low, mixed_low, preferred_element_type=jnp.float32)
    grad_mixed = jnp.einsum("to,oi->ti", grad_attn_low, out_all, preferred_element_type=jnp.float32)
    grad_mixed = grad_mixed.astype(jnp.bfloat16).reshape(local_rows, head_count, head_dim)
    probs_again = jnp.exp(attention_scores() - log_total)
    probs_again_low = probs_again.astype(jnp.bfloat16)
    grad_values = jnp.einsum(
        "hts,thd->shd", probs_again_low, grad_mixed, preferred_element_type=jnp.float32
    )
    grad_probs = jnp.einsum(
        "thd,shd->hts", grad_mixed, value_heads, preferred_element_type=jnp.float32
    )
    row_delta = jnp.sum(grad_probs * probs_again, axis=-1, keepdims=True)
    grad_scores = (score_scale * probs_again * (grad_probs - row_delta)).astype(jnp.bfloat16)
    grad_queries = jnp.einsum(
        "hts,shd->thd", grad_scores, key_heads, preferred_element_type=jnp.float32
    )
    grad_keys = jnp.einsum("hts,thd->shd", grad_scores, queries, preferred_element_type=jnp.float32)
    grad_key_own, grad_value_own = (
        lax.psum_scatter(
            grad_keys.reshape(seq_length, width).astype(jnp.bfloat16),
            "seq",
            scatter_dimension=0,
            tiled=True,
        ).astype(jnp.float32),
        lax.psum_scatter(
            grad_values.reshape(seq_length, width).astype(jnp.bfloat16),
            "seq",
            scatter_dimension=0,
            tiled=True,
        ).astype(jnp.float32),
    )
    grad_key_heads = grad_key_own.reshape(local_rows, head_count, head_dim)
    grad_query_raw = grad_queries * cosine - turned(grad_queries) * sine
    grad_key_raw = grad_key_heads * cosine - turned(grad_key_heads) * sine
    grad_qkv = jnp.concatenate(
        [
            grad_query_raw.reshape(local_rows, width),
            grad_key_raw.reshape(local_rows, width),
            grad_value_own,
        ],
        axis=-1,
    ).astype(jnp.bfloat16)
    grad_w_qkv = jnp.einsum("td,te->de", first_h, grad_qkv, preferred_element_type=jnp.float32)
    grad_first = jnp.einsum("te,de->td", grad_qkv, qkv_all, preferred_element_type=jnp.float32)
    grad_attn_gain = jnp.sum(grad_first * normed_one, axis=0)
    grad_inputs = grad_after + norm_back(
        grad_first * attn_gain_all.astype(jnp.float32), normed_one, inverse_one
    )
    grad_attn_gain_own, grad_qkv_own, grad_out_own, grad_ffn_gain_own, grad_router_own = (
        lax.psum_scatter(grad_attn_gain, ("dp", "seq"), scatter_dimension=0, tiled=True),
        lax.psum_scatter(grad_w_qkv, ("dp", "seq"), scatter_dimension=0, tiled=True),
        lax.psum_scatter(grad_out, ("dp", "seq"), scatter_dimension=0, tiled=True),
        lax.psum_scatter(grad_ffn_gain, ("dp", "seq"), scatter_dimension=0, tiled=True),
        lax.psum_scatter(grad_router, ("dp", "seq"), scatter_dimension=0, tiled=True),
    )
    return (
        outputs.astype(jnp.bfloat16),
        loss,
        grad_inputs,
        grad_attn_gain_own,
        grad_qkv_own,
        grad_out_own,
        grad_router_own,
        grad_ffn_gain_own,
        grad_gate_up_own,
        grad_down_own,
    )


def solution(mesh):
    in_specs = (
        P(("dp", "seq"), None),
        P(("dp", "seq"), None),
        P(),
        P(("dp", "seq"), None),
        P(("dp", "seq")),
        P(("dp", "seq"), None),
        P(("dp", "seq"), None),
        P(("dp", "seq"), None),
        P(("dp", "seq")),
        P("dp", None, None, "seq"),
        P("dp", None, "seq"),
    )
    out_specs = (
        P(("dp", "seq"), None),
        P(),
        P(("dp", "seq"), None),
        P(("dp", "seq")),
        P(("dp", "seq"), None),
        P(("dp", "seq"), None),
        P(("dp", "seq"), None),
        P(("dp", "seq")),
        P("dp", None, None, "seq"),
        P("dp", None, "seq"),
    )
    return jax.shard_map(
        on_device, mesh=mesh, in_specs=in_specs, out_specs=out_specs, check_vma=False
    )
```

profile of v0, /device:TPU:1, one launch (start us, length us, event | category | flops | bytes accessed | tf_op | source)
XLA Modules:
  0.0 1878.3 jit_solution(18438602625626763200)
XLA Ops:
  12.3 68.9 %all-reduce.10 = (bf16[1280]{0:T(1024)(128)(2,1)S(1)}, bf16[1280]{0:T(1024)(128)(2,1)S(1)}) all-reduce(bf16[1280]{0:T(1024)(128)(2,1)S(1)} %dynamic-update-slice, bf16[1280]{0:T(1024)(128)(2,1)S(1)} %dynamic-update-slice.1), channel_id=1, replica_groups=mesh['dp'=16,'seq'=8] {'dp','seq'}, use_global_device_ids=true, to_apply=%add.1 | all-reduce | flops 2560 | bytes 10240
  82.4 256.7 %all-gather.21.cloned.1.call-done = bf16[128,10,3840]{2,1,0:T(8,128)(2,1)} async-done(((bf16[1,10,3840]{2,1,0:T(8,128)(2,1)}), bf16[128,10,3840]{2,1,0:T(8,128)(2,1)}) %all-gather.21.cloned.1.call-update) | async-done | bytes 9830416 | tf_op jit(solution)/shard_map/all_gather | solution.py:66
  339.1 15.4 reshape.166
  372.6 20.8 %all-gather.15.cloned.1.call-done = bf16[80,4,2,896]{0,1,2,3:T(4,128)(2,1)} async-done(((bf16[80,4,2,112]{0,1,2,3:T(4,128)(2,1)}), bf16[80,4,2,896]{0,1,2,3:T(4,128)(2,1)}) %all-gather.15.cloned.1.call-update) | async-done | bytes 1146896 | tf_op jit(solution)/shard_map/all_gather | solution.py:114
  397.7 30.8 %all_gather.42 = bf16[80,4,896]{0,1,2:T(4,128)(2,1)S(1)} all-gather(bf16[80,4,112]{0,1,2:T(4,128)(2,1)S(1)} %copy.109), channel_id=1, replica_groups=mesh['dp'=16,'seq'=8] {'seq'}, dimensions={2}, use_global_device_ids=true | all-gather | bytes 645120 | tf_op jit(solution)/shard_map/all_gather | solution.py:115
  430.2 301.4 %all-gather.2 = bf16[128,10,3]{1,2,0:T(4,128)(2,1)S(1)} all-gather(bf16[1,10,3]{1,2,0:T(4,128)(2,1)S(1)} %bitcast.151), channel_id=1, replica_groups=mesh['dp'=16,'seq'=8] {'dp','seq'}, dimensions={0}, use_global_device_ids=true | all-gather | bytes 7740 | tf_op jit(solution)/shard_map/all_gather | solution.py:69
  744.8 19.2 %all-gather.11.cloned.1.call-done = bf16[1024,1280]{1,0:T(8,128)(2,1)} async-done(((bf16[128,1280]{1,0:T(8,128)(2,1)}), bf16[1024,1280]{1,0:T(8,128)(2,1)}) %all-gather.11.cloned.1.call-update) | async-done | bytes 2621456 | tf_op jit(solution)/shard_map/all_gather | solution.py:83
  768.6 54.6 %all-gather.13.cloned.1.call-done = bf16[1024,1280]{1,0:T(8,128)(2,1)} async-done(((bf16[128,1280]{1,0:T(8,128)(2,1)}), bf16[1024,1280]{1,0:T(8,128)(2,1)}) %all-gather.13.cloned.1.call-update) | async-done | bytes 2621456 | tf_op jit(solution)/shard_map/all_gather | solution.py:82
  839.7 82.6 %all-gather.17.cloned.1.call-done = bf16[1280,4,2,896]{3,0,2,1:T(8,128)(2,1)} async-done(((bf16[80,4,2,896]{3,0,2,1:T(8,128)(2,1)}), bf16[1280,4,2,896]{3,0,2,1:T(8,128)(2,1)}) %all-gather.17.cloned.1.call-update) | async-done | bytes 18350096 | tf_op jit(solution)/shard_map/all_gather | solution.py:118
  922.3 8.9 fusion.37
  934.4 46.3 %all-gather.19.cloned.1.call-done = bf16[1280,4,896]{2,0,1:T(8,128)(2,1)} async-done(((bf16[80,4,896]{2,0,1:T(8,128)(2,1)}), bf16[1280,4,896]{2,0,1:T(8,128)(2,1)}) %all-gather.19.cloned.1.call-update) | async-done | bytes 9175056 | tf_op jit(solution)/shard_map/all_gather | solution.py:119
  980.7 7.2 fusion.6
  991.8 13.7 convolution_bitcast_fusion
  1039.9 9.0 convolution_convert_fusion
  1058.1 43.4 %reduce-scatter.20.cloned.1.call-done = bf16[128,1280]{1,0:T(8,128)(2,1)} async-done(((bf16[1024,1280]{1,0:T(8,128)(2,1)}), bf16[128,1280]{1,0:T(8,128)(2,1)}) %reduce-scatter.20.cloned.1.call-update) | async-done | bytes 327696
  1103.9 77.8 %reduce-scatter.22.cloned.1.call-done = bf16[128,1280]{1,0:T(8,128)(2,1)} async-done(((bf16[1024,1280]{1,0:T(8,128)(2,1)}), bf16[128,1280]{1,0:T(8,128)(2,1)}) %reduce-scatter.22.cloned.1.call-update) | async-done | bytes 327696
  1182.9 9.4 fusion.34
  1192.4 95.8 %reduce-scatter.18.cloned.1.call-done = bf16[80,4,896]{2,0,1:T(8,128)(2,1)} async-done(((bf16[1280,4,896]{2,0,1:T(8,128)(2,1)}), bf16[80,4,896]{2,0,1:T(8,128)(2,1)}) %reduce-scatter.18.cloned.1.call-update) | async-done | bytes 573456 | tf_op jit(solution)/shard_map/reduce_scatter | solution.py:152
  1291.8 196.0 %reduce-scatter.16.cloned.1.call-done = bf16[80,4,2,896]{3,0,2,1:T(8,128)(2,1)} async-done(((bf16[1280,4,2,896]{3,0,2,1:T(8,128)(2,1)}), bf16[80,4,2,896]{3,0,2,1:T(8,128)(2,1)}) %reduce-scatter.16.cloned.1.call-update) | async-done | bytes 1146896 | tf_op jit(solution)/shard_map/reduce_scatter | solution.py:149
  1494.6 7.5 fusion.26
  1502.1 67.2 %all-reduce.8 = (f32[]{:T(128)}, f32[1280]{0:T(1024)S(1)}, f32[1280,3]{0,1:T(4,128)S(1)}, f32[1280]{0:T(1024)S(1)}) all-reduce(f32[]{:T(128)} %get-tuple-element.68, f32[1280]{0:T(1024)S(1)} %get-tuple-element.52, f32[1280,3]{0,1:T(4,128)S(1)} %fusion.61, f32[1280]{0:T(1024)S(1)} %get-tuple-element.50), channel_id=1, replica_groups=mesh['dp'=16,'seq'=8] {'dp','seq'}, use_global_device_ids=true, to_apply=%region_8.9 | all-reduce | flops 6401 | bytes 51208 | tf_op jit(solution)/shard_map/psum | solution.py:131
  1573.0 156.2 %all-reduce.13.cloned.1.call-done = (f32[1280,3840]{1,0:T(8,128)}, f32[1280,1280]{1,0:T(8,128)}) async-done(((f32[1280,3840]{1,0:T(8,128)}, f32[1280,1280]{1,0:T(8,128)}), (f32[1280,3840]{1,0:T(8,128)}, f32[1280,1280]{1,0:T(8,128)})) %all-reduce.13.cloned.1.call-update) | async-done | bytes 26214416
  1732.4 65.2 %reduce-scatter.26.cloned.1.call-done = bf16[112,320]{1,0:T(8,128)(2,1)} async-done(((bf16[896,320]{1,0:T(8,128)(2,1)}), bf16[112,320]{1,0:T(8,128)(2,1)}) %reduce-scatter.26.cloned.1.call-update) | async-done | bytes 71696
  1799.4 68.6 %reduce-scatter.24.cloned.1.call-done = bf16[112,640]{1,0:T(8,128)(2,1)} async-done(((bf16[896,640]{1,0:T(8,128)(2,1)}), bf16[112,640]{1,0:T(8,128)(2,1)}) %reduce-scatter.24.cloned.1.call-update) | async-done | bytes 143376
  (204 shorter events, 138.7 us)
Async XLA Ops:
  7.2 331.9 %all-gather.21.cloned.1.call-start = ((), (), s32[]{:S(2)}) async-start(), calls=%async_computation.13 | async-start | bytes 15851520 | tf_op jit(solution)/shard_map/all_gather | solution.py:66
  7.9 385.5 %all-gather.15.cloned.1.call-start = ((), (), s32[]{:S(2)}) async-start(), calls=%async_computation.8 | async-start | bytes 2064384 | tf_op jit(solution)/shard_map/all_gather | solution.py:114
  9.8 724.5 %all-gather.23.cloned.1.call-start = ((), (), s32[]{:S(2)}) async-start(), calls=%async_computation.14 | async-start | bytes 5283840 | tf_op jit(solution)/shard_map/all_gather | solution.py:67
  10.6 753.5 %all-gather.11.cloned.1.call-start = ((), (), s32[]{:S(2)}) async-start(), calls=%async_computation.6 | async-start | bytes 2949120 | tf_op jit(solution)/shard_map/all_gather | solution.py:83
  82.3 272.1 %copy-start.32 = (f32[128]{0:T(128)}, f32[128]{0:T(128)S(1)}, u32[]{:S(2)}) copy-start(f32[128]{0:T(128)S(1)} %add_rsqrt_fusion.1) | copy-start | bytes 1540
  82.3 272.1 %copy-start.11 = (bf16[128,1280]{1,0:T(8,128)(2,1)S(1)}, bf16[128,1280]{1,0:T(8,128)(2,1)}, u32[]{:S(2)}) copy-start(bf16[128,1280]{1,0:T(8,128)(2,1)} %param.11) | copy-start | bytes 983044
  360.6 462.6 %all-gather.13.cloned.1.call-start = ((), (), s32[]{:S(2)}) async-start(), calls=%async_computation.7 | async-start | bytes 2949120 | tf_op jit(solution)/shard_map/all_gather | solution.py:82
  372.5 25.0 %copy-start.31 = (bf16[80,4,112]{2,1,0:T(4,128)(2,1)S(1)}, bf16[80,4,112]{2,1,0:T(4,128)(2,1)}, u32[]{:S(2)}) copy-start(bf16[80,4,112]{2,1,0:T(4,128)(2,1)} %param.21) | copy-start | bytes 215044
  372.5 549.7 %all-gather.17.cloned.1.call-start = ((), (), s32[]{:S(2)}) async-start(), calls=%async_computation.9 | async-start | bytes 19496960 | tf_op jit(solution)/shard_map/all_gather | solution.py:118
  397.4 32.7 %copy-start.35 = (bf16[10,3]{0,1:T(4,128)(2,1)S(1)}, bf16[10,3]{0,1:T(4,128)(2,1)}, u32[]{:S(2)}) copy-start(bf16[10,3]{0,1:T(4,128)(2,1)} %param.18) | copy-start | bytes 184
  397.4 334.9 %copy-start.37 = (s32[16]{0:T(128)S(1)}, s32[16]{0:T(128)}, u32[]{:S(2)}) copy-start(s32[16]{0:T(128)} %param.13) | copy-start | bytes 196
  397.4 336.1 %copy-start.36 = (s32[128,2]{0,1:T(2,128)S(1)}, s32[128,2]{0,1:T(2,128)}, u32[]{:S(2)}) copy-start(s32[128,2]{0,1:T(2,128)} %param.14) | copy-start | bytes 3076
  397.5 583.3 %all-gather.19.cloned.1.call-start = ((), (), s32[]{:S(2)}) async-start(), calls=%async_computation.10 | async-start | bytes 9748480 | tf_op jit(solution)/shard_map/all_gather | solution.py:119
  430.1 671.4 %reduce-scatter.20.cloned.1.call-start = ((), (), s32[]{:S(2)}) async-start(), calls=%async_computation.15 | async-start | bytes 2949120
  1024.5 157.2 %reduce-scatter.22.cloned.1.call-start = ((), (), s32[]{:S(2)}) async-start(), calls=%async_computation.16 | async-start | bytes 2949120
  1030.8 257.4 %reduce-scatter.18.cloned.1.call-start = ((), (), s32[]{:S(2)}) async-start(), calls=%async_computation.12 | async-start | bytes 9748480 | tf_op jit(solution)/shard_map/reduce_scatter | solution.py:152
  1038.4 449.4 %reduce-scatter.16.cloned.1.call-start = ((), (), s32[]{:S(2)}) async-start(), calls=%async_computation.11 | async-start | bytes 19496960 | tf_op jit(solution)/shard_map/reduce_scatter | solution.py:149
  1048.9 680.2 %all-reduce.13.cloned.1.call-start = ((), (), s32[]{:S(2)}) async-start(), calls=%async_computation.19 | async-start | bytes 52428800
  1058.1 44.8 %copy-start.20 = (f32[128,10,128]{0,2,1:T(8,128)S(1)}, f32[128,10,128]{0,2,1:T(8,128)}, u32[]{:S(2)}) copy-start(f32[128,10,128]{0,2,1:T(8,128)} %copy-done.19) | copy-start | bytes 1966084
  1102.9 80.1 %copy-start.13 = (bf16[128,1280]{1,0:T(8,128)(2,1)S(1)}, bf16[128,1280]{1,0:T(8,128)(2,1)}, u32[]{:S(2)}) copy-start(bf16[128,1280]{1,0:T(8,128)(2,1)} %param.11) | copy-start | bytes 983044
  1102.9 80.1 %copy-start.33 = (f32[128]{0:T(128)S(1)}, f32[128]{0:T(128)}, u32[]{:S(2)}) copy-start(f32[128]{0:T(128)} %copy-done.32) | copy-start | bytes 1540
  1103.9 88.5 %copy-start.27 = (bf16[128,1280]{0,1:T(8,128)(2,1)}, bf16[128,1280]{0,1:T(8,128)(2,1)S(1)}, u32[]{:S(2)}) copy-start(bf16[128,1280]{0,1:T(8,128)(2,1)S(1)} %fusion.32) | copy-start | bytes 983044
  1192.4 605.2 %reduce-scatter.26.cloned.1.call-start = ((), (), s32[]{:S(2)}) async-start(), calls=%async_computation.18 | async-start | bytes 774144
  1291.7 576.3 %reduce-scatter.24.cloned.1.call-start = ((), (), s32[]{:S(2)}) async-start(), calls=%async_computation.17 | async-start | bytes 1290240
  (30 other events, 90.8 us)
Sparse Core Ops, SparseCore 0:
  9.7 329.3 all-gather.20
  341.9 51.4 all-gather.14
  395.1 308.9 all-gather.22
  706.8 57.1 all-gather.10
  766.8 56.3 all-gather.12
  824.7 97.5 all-gather.16
  923.9 56.7 all-gather.18
  1024.6 76.8 reduce-scatter.19
  1105.3 76.3 reduce-scatter.21
  1184.0 104.1 reduce-scatter.17
  1290.8 196.9 reduce-scatter.15
  1494.4 234.7 all-reduce.12
  1732.8 64.7 reduce-scatter.25
  1801.0 66.9 reduce-scatter.23
where the time goes:
time: 1890 us; the launch traced here: 1880 us
  waiting for transfers between devices  1180 us (62%)
  blocking collectives  468 us (25%)
  matrix products  95.7 us (5%)
  local copies, waits for them, and re-layouts  92.5 us (5%)
  other arithmetic  19.5 us (1%)
    unnamed x19, waiting for transfers between devices  413 us
    all_gather x1, blocking collectives, on_device(): lax.all_gather(router_w, ('dp', 'seq'), axis=0, tiled=True)  301 us
    all_gather x1, waiting for transfers between devices, on_device(): lax.all_gather(w_qkv, ('dp', 'seq'), axis=0, tiled=True)  257 us
    reduce_scatter x1, waiting for transfers between devices, on_device(): lax.psum_scatter(grad_w_gate_up.astype(jnp.bfloat16), 'dp', scatter_dimen...  196 us
    reduce_scatter x1, waiting for transfers between devices, on_device(): lax.psum_scatter(grad_down.astype(jnp.bfloat16), 'dp', scatter_dimension=...  95.8 us
    all_gather x1, waiting for transfers between devices, on_device(): lax.all_gather(gate_up_part, 'dp', axis=0, tiled=True)  82.6 us
    unnamed x1, blocking collectives  68.9 us
    psum x1, blocking collectives, on_device(): squares = lax.psum(jnp.sum(diff * diff), ('dp', 'seq'))  67.2 us
  transfers between devices with their start and end apart: 14, of which 13 were waited for; matrix products, arithmetic and copies ran while one was open for 8% of the time, Pallas kernels for 0%

commit v1 on v0

v1 whole, which is shorter than its diff:
```python
import functools

import jax
import jax.numpy as jnp
import numpy as np
from jax import lax
from jax.experimental import pallas as pl
from jax.experimental.pallas import tpu as pltpu
from jax.sharding import Mesh, PartitionSpec as P

D = 1280
HD = 128
HEADS = 10
SLOTS = 2
GROUPS = 5
HW = SLOTS * HD
QKV = 3 * HW
EXT = 128
WA = QKV + HW + EXT
ROWS = 128
SEQ = 1024
UNITS = 112
GU = 4 * 2 * 128
DN = 4 * 128
WM = GU + DN
norm_eps = 1e-06
masked_score = -1e30
rope_base = 10000.0
SCALE = HD ** (-0.5)
F32 = jnp.float32
BF16 = jnp.bfloat16
VMEM_LIMIT = 58 * 1024 * 1024

NT = (((1,), (1,)), ((), ()))
TN = (((0,), (0,)), ((), ()))


def dot(a, b):
    return jnp.dot(a, b, preferred_element_type=F32)


def dot_nt(a, b):
    return lax.dot_general(a, b, NT, preferred_element_type=F32)


def rows_of(start, count=ROWS):
    return pl.ds(pl.multiple_of(start, ROWS), count)


def half_turn(u):
    return pltpu.roll(u, HD // 2, 1)


def attn_fwd_kernel(info, *refs):
    xs = refs[:8]
    w, cos, sin = refs[8:11]
    a, b, h1, q, k, v, mixed, lse, ext, chosen = refs[11:21]
    part, vt = refs[21:]
    ext_t = w[:, QKV + HW : WA].astype(F32).T
    ext[...] = ext_t
    gain = ext_t[0:1, :]
    for i in range(8):
        blk = xs[i][:, :D].astype(F32)
        r = lax.rsqrt(jnp.mean(blk * blk, axis=1, keepdims=True) + norm_eps)
        at = rows_of(info[i] * ROWS)
        h1[at, :] = (blk * r * gain).astype(BF16)
        chosen[at, :] = xs[i][:, D:]

    @pl.loop(0, 4)
    def _(step):
        at = rows_of(step * 256, 256)
        full = dot(h1[at, :], w[:, :QKV])
        c, s = cos[at, :], sin[at, :]
        for j in range(SLOTS):
            col = slice(j * HD, (j + 1) * HD)
            u = full[:, j * HD : (j + 1) * HD]
            q[at, col] = (u * c + half_turn(u) * s).astype(BF16)
            u = full[:, HW + j * HD : HW + (j + 1) * HD]
            k[at, col] = (u * c + half_turn(u) * s).astype(BF16)
            u = full[:, 2 * HW + j * HD : 2 * HW + (j + 1) * HD]
            v[at, col] = u.astype(BF16)
            vt[col, at] = u.T.astype(BF16)

    prefix = info[16]
    lse[...] = jnp.zeros_like(lse)
    for j in range(SLOTS):
        col = slice(j * HD, (j + 1) * HD)

        @pl.loop(0, 4)
        def _(step, j=j, col=col):
            at = rows_of(step * 256, 256)
            s = dot_nt(k[:, col], q[at, col]) * SCALE
            key = lax.broadcasted_iota(jnp.int32, (SEQ, 256), 0)
            query = lax.broadcasted_iota(jnp.int32, (SEQ, 256), 1) + step * 256
            s = jnp.where(key < jnp.maximum(query + 1, prefix), s, masked_score)
            top = jnp.max(s, axis=0, keepdims=True)
            e = jnp.exp(s - top)
            total = jnp.sum(e, axis=0, keepdims=True)
            pn = (e * (1.0 / total)).astype(BF16)
            mixed[at, col] = dot(vt[col, :], pn).T.astype(BF16)
            lse[j : j + 1, at] = top + jnp.log(total)

    @pl.loop(0, 4)
    def _(step):
        at = rows_of(step * 256, 256)
        part[at, :] = dot_nt(mixed[at, :], w[:, QKV : QKV + HW]).astype(BF16)

    for i in range(4):
        out = slice(i * ROWS, (i + 1) * ROWS)
        a[out, :] = part[rows_of(info[8 + i] * ROWS), :]
        b[out, :] = part[rows_of(info[12 + i] * ROWS), :]


def moe_fwd_kernel(info, *refs):
    hs = refs[:8]
    w, wm, chosen = refs[8:11]
    a, b, h2, gu, z, comb = refs[11:17]
    (part,) = refs[17:]
    for i in range(8):
        h2[rows_of(info[i] * ROWS), :] = hs[i][...]

    @pl.loop(0, 4)
    def _(step):
        at = rows_of(step * 256, 256)
        h = h2[at, :]
        logits = dot(h, w[:, QKV + HW : WA])
        lane = lax.broadcasted_iota(jnp.int32, logits.shape, 1)
        live = (lane >= 2) & (lane < 5)
        logits = jnp.where(live, logits, masked_score)
        e = jnp.exp(logits - jnp.max(logits, axis=1, keepdims=True))
        gates = e / jnp.sum(e, axis=1, keepdims=True)
        cb = gates * chosen[at, :].astype(F32)
        comb[at, :] = cb
        full = dot(h, wm[:, :GU])
        gu[at, :] = full
        for x in range(4):
            gate = full[:, x * 256 : x * 256 + 128]
            up = full[:, x * 256 + 128 : x * 256 + 256]
            act = gate * jax.nn.sigmoid(gate) * up
            if x:
                act = act * cb[:, x + 1 : x + 2]
            z[at, x * 128 : (x + 1) * 128] = act.astype(BF16)
        part[at, :] = dot_nt(z[at, :], wm[:, GU:]).astype(BF16)

    for i in range(4):
        out = slice(i * ROWS, (i + 1) * ROWS)
        a[out, :] = part[rows_of(info[8 + i] * ROWS), :]
        b[out, :] = part[rows_of(info[12 + i] * ROWS), :]


def moe_bwd_kernel(info, *refs):
    ds = refs[:8]
    wm, gu, comb = refs[8:11]
    a, b, dm, dgu = refs[11:15]
    (part,) = refs[15:]
    for i in range(8):
        dm[rows_of(info[i] * ROWS), :] = ds[i][...]

    @pl.loop(0, 4)
    def _(step):
        at = rows_of(step * 256, 256)
        dz = dot(dm[at, :], wm[:, GU:])
        cb = comb[at, :]
        lane = lax.broadcasted_iota(jnp.int32, (256, 128), 1)
        extra = jnp.zeros((256, 128), F32)
        for x in range(4):
            gate = gu[at, x * 256 : x * 256 + 128]
            up = gu[at, x * 256 + 128 : x * 256 + 256]
            sig = jax.nn.sigmoid(gate)
            silu = gate * sig
            dact = dz[:, x * 128 : (x + 1) * 128]
            if x:
                dc = jnp.sum(dact * (silu * up), axis=1, keepdims=True)
                high = dc.astype(BF16).astype(F32)
                extra = jnp.where(lane == x + 1, high, extra)
                extra = jnp.where(lane == x + 4, dc - high, extra)
                dact = dact * cb[:, x + 1 : x + 2]
            dgu[at, x * 256 : x * 256 + 128] = (
                dact * up * sig * (1.0 + gate * (1.0 - sig))
            ).astype(BF16)
            dgu[at, x * 256 + 128 : x * 256 + 256] = (dact * silu).astype(BF16)
        part[at, :D] = dot_nt(dgu[at, :], wm[:, :GU]).astype(BF16)
        part[at, D:] = extra.astype(BF16)

    for i in range(4):
        out = slice(i * ROWS, (i + 1) * ROWS)
        a[out, :] = part[rows_of(info[8 + i] * ROWS), :]
        b[out, :] = part[rows_of(info[12 + i] * ROWS), :]


def attn_bwd_kernel(info, *refs):
    ds = refs[:8]
    w, cos, sin, h1, q, k, v, lse, ext = refs[8:17]
    a, b, da, dqkv, dgain = refs[17:22]
    part, dmix, kt, dk, dv = refs[22:]
    for i in range(8):
        da[rows_of(info[i] * ROWS), :] = ds[i][...]

    @pl.loop(0, 4)
    def _(step):
        at = rows_of(step * 256, 256)
        dmix[at, :] = dot(da[at, :], w[:, QKV : QKV + HW]).astype(BF16)
        for j in range(SLOTS):
            col = slice(j * HD, (j + 1) * HD)
            kt[col, at] = k[at, col].astype(F32).T.astype(BF16)

    prefix = info[16]
    for j in range(SLOTS):
        col = slice(j * HD, (j + 1) * HD)
        dk[...] = jnp.zeros_like(dk)
        dv[...] = jnp.zeros_like(dv)

        @pl.loop(0, 4)
        def _(step, j=j, col=col):
            at = rows_of(step * 256, 256)
            qb = q[at, col]
            s = dot_nt(k[:, col], qb) * SCALE
            key = lax.broadcasted_iota(jnp.int32, (SEQ, 256), 0)
            query = lax.broadcasted_iota(jnp.int32, (SEQ, 256), 1) + step * 256
            s = jnp.where(key < jnp.maximum(query + 1, prefix), s, masked_score)
            p = jnp.exp(s - lse[j : j + 1, at])
            dm = dmix[at, col]
            dv[...] += dot(p.astype(BF16), dm)
            dp = dot_nt(v[:, col], dm)
            delta = jnp.sum(dp * p, axis=0, keepdims=True)
            dsb = (SCALE * p * (dp - delta)).astype(BF16)
            dk[...] += dot(dsb, qb)
            dq = dot(kt[col, :], dsb).T
            c, sn = cos[at, :], sin[at, :]
            dqkv[at, col] = (dq * c - half_turn(dq) * sn).astype(BF16)

        u = dk[...]
        dqkv[:, HW + j * HD : HW + (j + 1) * HD] = (
            u * cos[...] - half_turn(u) * sin[...]
        ).astype(BF16)
        dqkv[:, 2 * HW + j * HD : 2 * HW + (j + 1) * HD] = dv[...].astype(BF16)

    dgain[...] = jnp.zeros_like(dgain)

    @pl.loop(0, 4)
    def _(step):
        at = rows_of(step * 256, 256)
        dh = dot_nt(dqkv[at, :], w[:, :QKV])
        part[at, :] = dh.astype(BF16)
        dgain[0:1, :] += jnp.sum(dh * h1[at, :].astype(F32), axis=0, keepdims=True)

    dgain[0:1, :] = dgain[0:1, :] / ext[0:1, :]
    for i in range(4):
        out = slice(i * ROWS, (i + 1) * ROWS)
        a[out, :] = part[rows_of(info[8 + i] * ROWS), :]
        b[out, :] = part[rows_of(info[12 + i] * ROWS), :]


def call(kernel, info, args, outs, scratch, flops):
    total = sum(int(np.prod(x.shape)) * x.dtype.itemsize for x in args)
    total += sum(int(np.prod(s)) * jnp.dtype(t).itemsize for s, t in outs)
    return pl.pallas_call(
        kernel,
        out_shape=[jax.ShapeDtypeStruct(s, t) for s, t in outs],
        in_specs=[pl.BlockSpec(memory_space=pltpu.SMEM)]
        + [pl.BlockSpec(memory_space=pltpu.VMEM)] * len(args),
        out_specs=[pl.BlockSpec(memory_space=pltpu.VMEM)] * len(outs),
        scratch_shapes=[pltpu.VMEM(s, t) for s, t in scratch],
        compiler_params=pltpu.CompilerParams(vmem_limit_bytes=VMEM_LIMIT),
        cost_estimate=pl.CostEstimate(flops=flops, bytes_accessed=total, transcendentals=0),
    )(info, *args)


def exchange(x):
    return lax.ppermute(x, ("c", "xh"), [(0, 0), (1, 2), (2, 1), (3, 3)])


def along_z(x, k):
    return lax.ppermute(x, "z", [(i, (i + k) % 4) for i in range(4)])


def to_other_core(x):
    return lax.ppermute(x, "c", [(0, 1), (1, 0)])


def gather_group(x):
    own = [x] + [along_z(x, k) for k in (1, 2, 3)]
    return own + [to_other_core(part) for part in own]


def scatter_group(a, b):
    got = to_other_core(b)
    s = [
        (a[i * ROWS : (i + 1) * ROWS].astype(F32) + got[i * ROWS : (i + 1) * ROWS].astype(F32))
        for i in range(4)
    ]
    total = s[0]
    for k in (1, 2, 3):
        total = total + along_z(s[k].astype(BF16), k).astype(F32)
    return total


PLANE = ("y", "xl", "xh")


def rope_tables():
    places = jnp.arange(SEQ, dtype=jnp.int32).astype(F32)
    half = HD // 2
    speeds = rope_base ** (-jnp.arange(half, dtype=F32) / half)
    angles = places[:, None] * speeds[None, :]
    c, s = jnp.cos(angles), jnp.sin(angles)
    return jnp.concatenate([c, c], axis=1), jnp.concatenate([-s, s], axis=1)


def on_device(
    tokens, teacher, prefix, routes, attn_gain, w_qkv, w_out, router_w, ffn_gain, w_gate_up, w_down
):
    core, zz = lax.axis_index("c"), lax.axis_index("z")
    near = [core * 4 + (zz + k) % 4 for k in range(4)]
    far = [(1 - core) * 4 + (zz + k) % 4 for k in range(4)]
    back = [0, 3, 2, 1]
    sequence = lax.axis_index(PLANE)
    info = jnp.stack(
        [near[i] for i in back] + [far[i] for i in back] + near + far + [prefix[sequence]]
    ).astype(jnp.int32)

    lanes = jnp.arange(EXT, dtype=jnp.int32)[None, :]
    chosen = (routes[:, 0:1] + 2 == lanes) | (routes[:, 1:2] + 2 == lanes)
    x_all = exchange(jnp.concatenate([tokens, chosen.astype(BF16)], axis=1))
    small = jnp.concatenate([attn_gain[:, None], ffn_gain[:, None], router_w], axis=1)
    raw = exchange(
        jnp.concatenate([w_qkv, w_out, jnp.pad(small, ((0, 0), (0, EXT - 5)))], axis=1)
    )
    n = raw.shape[0]
    heads = raw[:, : 4 * D].reshape(n, 4, GROUPS, HW).transpose(2, 0, 1, 3)
    heads = heads.reshape(GROUPS, n, 4 * HW)
    heads = jnp.pad(heads, ((0, 8 - GROUPS), (0, 0), (0, 0)))
    packed = jnp.concatenate(
        [heads, jnp.broadcast_to(raw[None, :, 4 * D :], (8, n, EXT))], axis=2
    )
    packed = lax.all_to_all(packed, ("c", "z"), split_axis=0, concat_axis=0)
    w = lax.all_gather(packed.reshape(8 * n, WA), PLANE, axis=0, tiled=True)
    lane_pad = 128 - UNITS
    wm_own = jnp.concatenate(
        [
            jnp.pad(w_gate_up, ((0, 0), (0, 0), (0, 0), (0, lane_pad))).reshape(-1, GU),
            jnp.pad(w_down, ((0, 0), (0, 0), (0, lane_pad))).reshape(-1, DN),
        ],
        axis=1,
    )
    wm = lax.all_gather(exchange(wm_own), PLANE, axis=0, tiled=True)
    teach = exchange(teacher)
    cos, sin = rope_tables()

    (a, b, h1, q, k, v, mixed, lse, ext, chosen_all) = call(
        attn_fwd_kernel,
        info,
        gather_group(x_all) + [w, cos, sin],
        [
            ((512, D), BF16),
            ((512, D), BF16),
            ((SEQ, D), BF16),
            ((SEQ, HW), BF16),
            ((SEQ, HW), BF16),
            ((SEQ, HW), BF16),
            ((SEQ, HW), BF16),
            ((8, SEQ), F32),
            ((EXT, D), F32),
            ((SEQ, EXT), BF16),
        ],
        [((SEQ, D), BF16), ((HW, SEQ), BF16)],
        4_000_000_000,
    )
    x = x_all[:, :D].astype(F32)
    x1 = x + scatter_group(a, b)
    r2 = lax.rsqrt(jnp.mean(x1 * x1, axis=1, keepdims=True) + norm_eps)
    n2 = x1 * r2
    gain_two = ext[1:2, :]
    h2 = (n2 * gain_two).astype(BF16)

    a, b, h2_all, gu, z, comb = call(
        moe_fwd_kernel,
        info,
        gather_group(h2) + [w, wm, chosen_all],
        [
            ((512, D), BF16),
            ((512, D), BF16),
            ((SEQ, D), BF16),
            ((SEQ, GU), F32),
            ((SEQ, DN), BF16),
            ((SEQ, EXT), F32),
        ],
        [((SEQ, D), BF16)],
        4_000_000_000,
    )
    y = x1 + scatter_group(a, b)
    diff = y - teach.astype(F32)
    squares = jnp.sum(diff * diff)
    dm = diff.astype(BF16)
    a, b, dm_all, dgu = call(
        moe_bwd_kernel,
        info,
        gather_group(dm) + [wm, gu, comb],
        [((512, D + EXT), BF16), ((512, D + EXT), BF16), ((SEQ, D), BF16), ((SEQ, GU), BF16)],
        [((SEQ, D + EXT), BF16)],
        4_000_000_000,
    )
    dwm = jnp.concatenate(
        [
            lax.dot_general(h2_all, dgu, TN, preferred_element_type=F32).astype(BF16),
            lax.dot_general(dm_all, z, TN, preferred_element_type=F32).astype(BF16),
        ],
        axis=1,
    )
    dwm_own = exchange(lax.psum_scatter(dwm, PLANE, scatter_dimension=0, tiled=True))
    dh2 = scatter_group(a, b)
    dcomb = dh2[:, D + 2 : D + 5] + dh2[:, D + 5 : D + 8]
    router = ext[2:5, :].astype(BF16)
    logits = lax.dot_general(h2, router, NT, preferred_element_type=F32)
    gates = jax.nn.softmax(logits, axis=1)
    dpick = dcomb * x_all[:, D + 2 : D + 5].astype(F32)
    dlogits = (gates * (dpick - jnp.sum(dpick * gates, axis=1, keepdims=True))).astype(BF16)
    d_router = lax.dot_general(dlogits, h2, TN, preferred_element_type=F32)
    dh2 = dh2[:, :D] + jnp.dot(dlogits, router, preferred_element_type=F32)
    d_ffn_gain = jnp.sum(dh2 * n2, axis=0, keepdims=True)
    g2 = dh2 * gain_two
    dx1 = diff + r2 * (g2 - n2 * jnp.mean(g2 * n2, axis=1, keepdims=True))
    da = dx1.astype(BF16)

    a, b, da_all, dqkv, dgain = call(
        attn_bwd_kernel,
        info,
        gather_group(da) + [w, cos, sin, h1, q, k, v, lse, ext],
        [
            ((512, D), BF16),
            ((512, D), BF16),
            ((SEQ, D), BF16),
            ((SEQ, QKV), BF16),
            ((8, D), F32),
        ],
        [
            ((SEQ, D), BF16),
            ((SEQ, HW), BF16),
            ((HW, SEQ), BF16),
            ((SEQ, HD), F32),
            ((SEQ, HD), F32),
        ],
        6_000_000_000,
    )
    sums = jnp.concatenate(
        [dgain[0:1], d_ffn_gain, d_router, jnp.full((1, D), squares / (SEQ * 16), F32)], axis=0
    )
    sums = jnp.pad(sums, ((0, EXT - 6), (0, 0))).T
    dw = jnp.concatenate(
        [
            lax.dot_general(h1, dqkv, TN, preferred_element_type=F32).astype(BF16),
            lax.dot_general(da_all, mixed, TN, preferred_element_type=F32).astype(BF16),
            sums.astype(BF16),
        ],
        axis=1,
    )
    dw = lax.psum_scatter(dw, PLANE, scatter_dimension=0, tiled=True)
    dw = lax.all_to_all(dw.reshape(8, n, WA), ("c", "z"), split_axis=0, concat_axis=0)
    dw_heads = dw[:GROUPS, :, : 4 * HW].reshape(GROUPS, n, 4, HW).transpose(1, 2, 0, 3)
    dw_small = jnp.sum(dw[:, :, 4 * HW :].astype(F32), axis=0)
    d_raw = exchange(
        jnp.concatenate([dw_heads.reshape(n, 4 * D), dw_small.astype(BF16)], axis=1)
    ).astype(F32)

    dh1 = scatter_group(a, b)
    r1 = lax.rsqrt(jnp.mean(x * x, axis=1, keepdims=True) + norm_eps)
    n1 = x * r1
    g1 = dh1 * ext[0:1, :]
    d_tokens = dx1 + r1 * (g1 - n1 * jnp.mean(g1 * n1, axis=1, keepdims=True))

    d_gu = dwm_own[:, :GU].reshape(-1, 4, 2, 128)[..., :UNITS].astype(F32)
    d_dn = dwm_own[:, GU:].reshape(-1, 4, 128)[..., :UNITS].astype(F32)
    return (
        exchange(y.astype(BF16)),
        d_raw[0, 4 * D + 5],
        exchange(d_tokens.astype(BF16)).astype(F32),
        d_raw[:, 4 * D],
        d_raw[:, : 3 * D],
        d_raw[:, 3 * D : 4 * D],
        d_raw[:, 4 * D + 2 : 4 * D + 5],
        d_raw[:, 4 * D + 1],
        d_gu,
        d_dn,
    )


def solution(mesh):
    fine = Mesh(mesh.devices.reshape(4, 2, 2, 2, 4), ("y", "xl", "c", "xh", "z"))
    every = ("y", "xl", "c", "xh", "z")
    rows = P(every, None)
    in_specs = (
        rows,
        rows,
        P(),
        rows,
        P(every),
        rows,
        rows,
        rows,
        P(every),
        P(("y", "xl", "c"), None, None, ("xh", "z")),
        P(("y", "xl", "c"), None, ("xh", "z")),
    )
    out_specs = (
        rows,
        P(),
        rows,
        P(every),
        rows,
        rows,
        rows,
        P(every),
        P(("y", "xl", "c"), None, None, ("xh", "z")),
        P(("y", "xl", "c"), None, ("xh", "z")),
    )
    return jax.shard_map(
        on_device, mesh=fine, in_specs=in_specs, out_specs=out_specs, check_vma=False
    )
```

time: 1890 us -> 627 us (0.33)
  waiting for transfers between devices: 1180 us -> 332 us
  blocking collectives: 468 us -> 12.6 us
  starting transfers between devices: 0.57 us -> 115 us
  matrix products: 95.7 us -> 13.2 us
  Pallas kernels: 0 us -> 70.4 us
  local copies, waits for them, and re-layouts: 92.5 us -> 31.3 us
    all_gather x7 -> x2, waiting for transfers between devices: 480 us -> 78.6 us  [the longest x1 47.3 us: on_device(): w = lax.all_gather(packed.reshape(8 * n, WA), PLANE, axis=0, tiled=True)]
    all_gather x2 -> x0, blocking collectives: 332 us -> none  [the longest x1 301 us: on_device(): lax.all_gather(router_w, ('dp', 'seq'), axis=0, tiled=True)]
    unnamed x19 -> x5, waiting for transfers between devices: 413 us -> 88.4 us
    reduce_scatter x2 -> x1, waiting for transfers between devices: 292 us -> 45 us  [on_device(): dw = lax.psum_scatter(dw, PLANE, scatter_dimension=0, tiled=True)]
    ppermute x0 -> x52, waiting for transfers between devices: none -> 120 us  [the longest x24 90.9 us: along_z(): return lax.ppermute(x, 'z', [(i, (i + k) % 4) for i in range(4)])]
    ppermute x0 -> x52, starting transfers between devices: none -> 98 us  [the longest x8 38.6 us: exchange(): return lax.ppermute(x, ('c', 'xh'), [(0, 0), (1, 2), (2, 1), (3, 3)])]
    dot_general x21 -> x7, matrix products: 95.7 us -> 13.2 us  [the longest x1 3.81 us: on_device(): lax.dot_general(h1, dqkv, TN, preferred_element_type=F32).astype(BF16)]
    pallas_call x0 -> x4, Pallas kernels: none -> 70.4 us  [call(): pl.pallas_call(kernel, out_shape=[jax.ShapeDtypeStruct(s, t) for s, t in...]
  transfers between devices with their start and end apart: 14 -> 57, of which waited for: 13 -> 35; matrix products, arithmetic and copies ran while one was open for 8% -> 6% of each run, Pallas kernels for 0% -> 3%
where the time goes in v1:
time: 627 us; the launch traced here: 616 us
  waiting for transfers between devices  332 us (53%)
  starting transfers between devices  115 us (18%)
  Pallas kernels  70.4 us (11%)
  local copies, waits for them, and re-layouts  31.3 us (5%)
  other arithmetic  25.4 us (4%)
  between operations  15.8 us (3%)
  matrix products  13.2 us (2%)
  blocking collectives  12.6 us (2%)
    ppermute x24, waiting for transfers between devices, along_z(): return lax.ppermute(x, 'z', [(i, (i + k) % 4) for i in range(4)])  90.9 us
    unnamed x5, waiting for transfers between devices  88.4 us
    pallas_call x4, Pallas kernels, call(): pl.pallas_call(kernel, out_shape=[jax.ShapeDtypeStruct(s, t) for s, t in...  70.4 us
    all_gather x1, waiting for transfers between devices, on_device(): w = lax.all_gather(packed.reshape(8 * n, WA), PLANE, axis=0, tiled=True)  47.3 us
    reduce_scatter x1, waiting for transfers between devices, on_device(): dw = lax.psum_scatter(dw, PLANE, scatter_dimension=0, tiled=True)  45 us
    ppermute x8, starting transfers between devices, exchange(): return lax.ppermute(x, ('c', 'xh'), [(0, 0), (1, 2), (2, 1), (3, 3)])  38.6 us
    ppermute x24, starting transfers between devices, along_z(): return lax.ppermute(x, 'z', [(i, (i + k) % 4) for i in range(4)])  33.2 us
    all_gather x1, waiting for transfers between devices, on_device(): wm = lax.all_gather(exchange(wm_own), PLANE, axis=0, tiled=True)  31.3 us
  transfers between devices with their start and end apart: 57, of which 35 were waited for; matrix products, arithmetic and copies ran while one was open for 6% of the time, Pallas kernels for 3%

profile of v1, /device:TPU:1, one launch (start us, length us, event | category | flops | bytes accessed | tf_op | source)
XLA Modules:
  0.0 615.5 jit_solution(11069131301235837237)
XLA Ops:
  9.1 6.0 collective-permute-start.8
  18.5 12.6 %all_to_all.10 = bf16[8,10,1152]{2,1,0:T(8,128)(2,1)S(1)} all-to-all(bf16[8,10,1152]{2,1,0:T(8,128)(2,1)S(1)} %fusion.10), channel_id=1, replica_groups=mesh['y'=4,'xl'=2,'c'=2,'xh'=2,'z'=4] {'c','z'}, dimensions={0} | all-to-all | bytes 368640 | tf_op jit(solution)/shard_map/all_to_all | solution.py:336
  42.6 5.9 collective-permute-start
  48.5 7.4 %collective-permute-done.refs_0_ = bf16[128,1408]{1,0:T(8,128)(2,1)S(1)} collective-permute-done((bf16[128,1408]{1,0:T(8,128)(2,1)S(1)}, bf16[128,1408]{1,0:T(8,128)(2,1)S(1)}, u32[]{:S(2)}, u32[]{:S(2)}) %collective-permute-start) | collective-permute-done | bytes 360480 | tf_op jit(solution)/shard_map/ppermute | solution.py:270
  60.5 7.1 %collective-permute-done.1.refs_1_ = bf16[128,1408]{1,0:T(8,128)(2,1)S(1)} collective-permute-done((bf16[128,1408]{1,0:T(8,128)(2,1)S(1)}, bf16[128,1408]{1,0:T(8,128)(2,1)S(1)}, u32[]{:S(2)}, u32[]{:S(2)}) %collective-permute-start.1) | collective-permute-done | bytes 360480 | tf_op jit(solution)/shard_map/ppermute | solution.py:274
  71.6 47.3 %all-gather.3.cloned.1.call-done.refs_8_ = bf16[1280,1152]{1,0:T(8,128)(2,1)} async-done(((bf16[80,1152]{1,0:T(8,128)(2,1)}), bf16[1280,1152]{1,0:T(8,128)(2,1)}) %all-gather.3.cloned.1.call-update) | async-done | bytes 2949136 | tf_op jit(solution)/shard_map/all_gather | solution.py:337
  118.9 20.1 %shard_map.186 = (bf16[512,1280]{1,0:T(8,128)(2,1)}, bf16[512,1280]{1,0:T(8,128)(2,1)}, bf16[1024,1280]{1,0:T(8,128)(2,1)}, bf16[1024,256]{1,0:T(8,128)(2,1)}, b...) custom-call(s32[17]{0:T(128)} %stack.43.info, ...), custom_call_target="tpu_custom_call" | custom-call | flops 4000000000 | bytes 15171584 | tf_op jit(solution)/shard_map/pallas_call | solution.py:257
  159.1 9.2 %collective-permute-done.11 = bf16[128,1280]{1,0:T(8,128)(2,1)S(1)} collective-permute-done((bf16[128,1280]{1,0:T(8,128)(2,1)S(1)}, bf16[128,1280]{1,0:T(8,128)(2,1)S(1)}, u32[]{:S(2)}, u32[]{:S(2)}) %collective-permute-start.11) | collective-permute-done | bytes 327712 | tf_op jit(solution)/shard_map/ppermute | solution.py:274
  181.3 6.8 %collective-permute-done.14.refs_2_ = bf16[128,1280]{1,0:T(8,128)(2,1)S(1)} collective-permute-done((bf16[128,1280]{1,0:T(8,128)(2,1)S(1)}, bf16[128,1280]{1,0:T(8,128)(2,1)S(1)}, u32[]{:S(2)}, u32[]{:S(2)}) %collective-permute-start.14) | collective-permute-done | bytes 327712 | tf_op jit(solution)/shard_map/ppermute | solution.py:274
  189.4 31.3 %all-gather.5.cloned.1.call-done.refs_9_.refs_8_ = bf16[1280,1536]{1,0:T(8,128)(2,1)} async-done(((bf16[80,1536]{1,0:T(8,128)(2,1)}), bf16[1280,1536]{1,0:T(8,128)(2,1)}) %all-gather.5.cloned.1.call-update) | async-done | bytes 3932176 | tf_op jit(solution)/shard_map/all_gather | solution.py:346
  221.6 14.7 %shard_map.187 = (bf16[512,1280]{1,0:T(8,128)(2,1)}, bf16[512,1280]{1,0:T(8,128)(2,1)}, bf16[1024,1280]{1,0:T(8,128)(2,1)}, f32[1024,1024]{1,0:T(8,128)}, bf16[1...) custom-call(s32[17]{0:T(128)} %stack.43.info, bf16[128,1280]{1,0:T(8,128)(2,1)} %copy-done.2, bf16[128,1280]{1,0:T(8,128)(2,1)} %copy-done.29, ...), custom_call_target="tpu_custom_call" | custom-call | flops 4000000000 | bytes 20774912 | tf_op jit(solution)/shard_map/pallas_call | solution.py:257
  251.9 13.1 %collective-permute-done.22 = bf16[128,1280]{1,0:T(8,128)(2,1)S(1)} collective-permute-done((bf16[128,1280]{1,0:T(8,128)(2,1)S(1)}, bf16[128,1280]{1,0:T(8,128)(2,1)S(1)}, u32[]{:S(2)}, u32[]{:S(2)}) %collective-permute-start.22) | collective-permute-done | bytes 327712 | tf_op jit(solution)/shard_map/ppermute | solution.py:274
  279.6 6.3 %collective-permute-done.28.refs_2_ = bf16[128,1280]{1,0:T(8,128)(2,1)S(1)} collective-permute-done((bf16[128,1280]{1,0:T(8,128)(2,1)S(1)}, bf16[128,1280]{1,0:T(8,128)(2,1)S(1)}, u32[]{:S(2)}, u32[]{:S(2)}) %collective-permute-start.28) | collective-permute-done | bytes 327712 | tf_op jit(solution)/shard_map/ppermute | solution.py:274
  289.7 13.0 %shard_map.188 = (bf16[512,1408]{1,0:T(8,128)(2,1)}, bf16[512,1408]{1,0:T(8,128)(2,1)}, bf16[1024,1280]{1,0:T(8,128)(2,1)}, bf16[1024,1024]{1,0:T(8,128)(2,1)}) custom-call(s32[17]{0:T(128)} %stack.43.info, bf16[128,1280]{1,0:T(8,128)(2,1)} %copy-done.8, bf16[128,1280]{1,0:T(8,128)(2,1)} %copy-done.31, bf16[128,1280]{1,0:T(8,128)(2,1)} %copy-done.34, ...), custom_call_target="tpu_custom_call" | custom-call | flops 4000000000 | bytes 18874368 | tf_op jit(solution)/shard_map/pallas_call | solution.py:257
  314.4 6.3 %collective-permute-done.35 = bf16[128,1408]{1,0:T(8,128)(2,1)S(1)} collective-permute-done((bf16[128,1408]{1,0:T(8,128)(2,1)}, bf16[128,1408]{1,0:T(8,128)(2,1)S(1)}, u32[]{:S(2)}, u32[]{:S(2)}) %collective-permute-start.35) | collective-permute-done | bytes 360480 | tf_op jit(solution)/shard_map/ppermute | solution.py:274
  320.7 8.0 %collective-permute-done.36 = bf16[128,1408]{1,0:T(8,128)(2,1)S(1)} collective-permute-done((bf16[128,1408]{1,0:T(8,128)(2,1)}, bf16[128,1408]{1,0:T(8,128)(2,1)S(1)}, u32[]{:S(2)}, u32[]{:S(2)}) %collective-permute-start.36) | collective-permute-done | bytes 360480 | tf_op jit(solution)/shard_map/ppermute | solution.py:274
  345.1 6.9 %collective-permute-done.39.refs_2_ = bf16[128,1280]{1,0:T(8,128)(2,1)S(1)} collective-permute-done((bf16[128,1280]{1,0:T(8,128)(2,1)S(1)}, bf16[128,1280]{1,0:T(8,128)(2,1)S(1)}, u32[]{:S(2)}, u32[]{:S(2)}) %collective-permute-start.39) | collective-permute-done | bytes 327712 | tf_op jit(solution)/shard_map/ppermute | solution.py:274
  355.7 22.7 %shard_map.189 = (bf16[512,1280]{1,0:T(8,128)(2,1)}, bf16[512,1280]{1,0:T(8,128)(2,1)}, bf16[1024,1280]{1,0:T(8,128)(2,1)}, bf16[1024,768]{1,0:T(8,128)(2,1)}, f32[8,1280]{1,0:T(8,128)}) custom-call(s32[17]{0:T(128)} %stack.43.info, bf16[128,1280]{1,0:T(8,128)(2,1)} %copy-done.10, bf16[128,1280]{1,0:T(8,128)(2,1)} %copy-done.24, ...), custom_call_target="tpu_custom_call" | custom-call | flops 6000000000 | bytes 18358272 | tf_op jit(solution)/shard_map/pallas_call | solution.py:257
  397.7 6.3 %copy.73 = bf16[1280,1536]{1,0:T(8,128)(2,1)} copy(bf16[1280,1536]{0,1:T(8,128)(2,1)} %pad_maximum_fusion) | data formatting | bytes 7864320
  419.0 6.8 %collective-permute-done.48 = bf16[128,1280]{1,0:T(8,128)(2,1)S(1)} collective-permute-done((bf16[128,1280]{1,0:T(8,128)(2,1)S(1)}, bf16[128,1280]{1,0:T(8,128)(2,1)S(1)}, u32[]{:S(2)}, u32[]{:S(2)}) %collective-permute-start.48) | collective-permute-done | bytes 327712 | tf_op jit(solution)/shard_map/ppermute | solution.py:274
  426.7 45.0 %reduce-scatter.7.cloned.1.call-done = bf16[80,1152]{1,0:T(8,128)(2,1)} async-done(((bf16[1280,1152]{1,0:T(8,128)(2,1)}), bf16[80,1152]{1,0:T(8,128)(2,1)}) %reduce-scatter.7.cloned.1.call-update) | async-done | bytes 184336 | tf_op jit(solution)/shard_map/reduce_scatter | solution.py:457
  473.4 16.6 %all-to-all-start.1 = ((bf16[8,10,1152]{2,1,0:T(8,128)(2,1)}), bf16[8,10,1152]{2,1,0:T(8,128)(2,1)}, u32[]{:S(2)}, u32[]{:S(2)}) async-start(bf16[8,10,1152]{2,1,0:T(8,128)(2,1)} %reshape.93), calls=%async_computation.1 | async-start | bytes 589824 | tf_op jit(solution)/shard_map/all_to_all | solution.py:458
  494.0 88.4 %reduce-scatter.9.cloned.1.call-done = bf16[80,1536]{1,0:T(8,128)(2,1)} async-done(((bf16[1280,1536]{1,0:T(8,128)(2,1)}), bf16[80,1536]{1,0:T(8,128)(2,1)}) %reduce-scatter.9.cloned.1.call-update) | async-done | bytes 245776
  583.6 9.7 %collective-permute-start.51 = (bf16[80,1536]{0,1:T(8,128)(2,1)S(1)}, bf16[80,1536]{0,1:T(8,128)(2,1)S(1)}, u32[]{:S(2)}, u32[]{:S(2)}) collective-permute-start(bf16[80,1536]{0,1:T(8,128)(2,1)S(1)} %copy.74), channel_id=1, source_target_pairs={{0,0},{4,8},{8,4},{12,12},{1,1},{5,9},{9,5},{13,13},{2,2},{6,10},{... | collective-permute-start | bytes 737288 | tf_op jit(solution)/shard_map/ppermute | solution.py:270
  (288 shorter events, 182.5 us)
Async XLA Ops:
  7.2 111.7 %all-gather.3.cloned.1.call-start = ((), (), s32[]{:S(2)}) async-start(), calls=%async_computation.4 | async-start | bytes 3133440 | tf_op jit(solution)/shard_map/all_gather | solution.py:337
  31.9 188.8 %all-gather.5.cloned.1.call-start = ((), (), s32[]{:S(2)}) async-start(), calls=%async_computation.5 | async-start | bytes 4177920 | tf_op jit(solution)/shard_map/all_gather | solution.py:346
  42.4 429.4 %reduce-scatter.7.cloned.1.call-start = ((), (), s32[]{:S(2)}) async-start(), calls=%async_computation.6 | async-start | bytes 3133440 | tf_op jit(solution)/shard_map/reduce_scatter | solution.py:457
  149.5 18.9 %collective-permute-start.11 = (bf16[128,1280]{1,0:T(8,128)(2,1)S(1)}, bf16[128,1280]{1,0:T(8,128)(2,1)S(1)}, u32[]{:S(2)}, u32[]{:S(2)}) collective-permute-start(bf16[128,1280]{1,0:T(8,128)(2,1)S(1)} %get-tuple-element.143), channel_id=1, source_target_pairs={{0,2},{1,3},{2,0},{3,1},{4,6},{5,7},{6,4},{7,5},{8,10},{9,11},{10,... | collective-permute-start | bytes 983048 | tf_op jit(solution)/shard_map/ppermute | solution.py:274
  170.6 17.5 %collective-permute-start.14 = (bf16[128,1280]{1,0:T(8,128)(2,1)S(1)}, bf16[128,1280]{1,0:T(8,128)(2,1)S(1)}, u32[]{:S(2)}, u32[]{:S(2)}) collective-permute-start(bf16[128,1280]{1,0:T(8,128)(2,1)S(1)} %multiply_convert_fusion.refs_0_), channel_id=1, source_target_pairs={{0,2},{1,3},{2,0},{3,1},{4,6},{5,7},{6,4},{7,5},{8,10},{9,11},{10,... | collective-permute-start | bytes 983048 | tf_op jit(solution)/shard_map/ppermute | solution.py:274
  173.6 15.7 %collective-permute-start.15 = (bf16[128,1280]{1,0:T(8,128)(2,1)S(1)}, bf16[128,1280]{1,0:T(8,128)(2,1)S(1)}, u32[]{:S(2)}, u32[]{:S(2)}) collective-permute-start(bf16[128,1280]{1,0:T(8,128)(2,1)S(1)} %multiply_convert_fusion.refs_0_), channel_id=1, source_target_pairs={{0,3},{1,0},{2,1},{3,2},{4,7},{5,4},{6,5},{7,6},{8,11},{9,8},{10,9... | collective-permute-start | bytes 983048 | tf_op jit(solution)/shard_map/ppermute | solution.py:274
  174.7 45.9 %collective-permute-start.16 = (bf16[128,1280]{1,0:T(8,128)(2,1)S(1)}, bf16[128,1280]{1,0:T(8,128)(2,1)S(1)}, u32[]{:S(2)}, u32[]{:S(2)}) collective-permute-start(bf16[128,1280]{1,0:T(8,128)(2,1)S(1)} %multiply_convert_fusion.refs_0_), channel_id=1, source_target_pairs={{0,8},{8,0},{1,9},{9,1},{2,10},{10,2},{3,11},{11,3},{4,12},{12,4},... | collective-permute-start | bytes 983048 | tf_op jit(solution)/shard_map/ppermute | solution.py:278
  179.7 40.9 %collective-permute-start.17 = (bf16[128,1280]{1,0:T(8,128)(2,1)S(1)}, bf16[128,1280]{1,0:T(8,128)(2,1)S(1)}, u32[]{:S(2)}, u32[]{:S(2)}) collective-permute-start(bf16[128,1280]{1,0:T(8,128)(2,1)S(1)} %collective-permute-done.13.refs_1_), channel_id=1, source_target_pairs={{0,8},{8,0},{1,9},{9,1},{2,10},{10,2},{3,11},{11,3},{4,12},{12,4},... | collective-permute-start | bytes 983048 | tf_op jit(solution)/shard_map/ppermute | solution.py:278
  188.1 32.6 %collective-permute-start.18 = (bf16[128,1280]{1,0:T(8,128)(2,1)S(1)}, bf16[128,1280]{1,0:T(8,128)(2,1)S(1)}, u32[]{:S(2)}, u32[]{:S(2)}) collective-permute-start(bf16[128,1280]{1,0:T(8,128)(2,1)S(1)} %collective-permute-done.14.refs_2_), channel_id=1, source_target_pairs={{0,8},{8,0},{1,9},{9,1},{2,10},{10,2},{3,11},{11,3},{4,12},{12,4},... | collective-permute-start | bytes 983048 | tf_op jit(solution)/shard_map/ppermute | solution.py:278
  189.3 31.4 %collective-permute-start.19 = (bf16[128,1280]{1,0:T(8,128)(2,1)S(1)}, bf16[128,1280]{1,0:T(8,128)(2,1)}, u32[]{:S(2)}, u32[]{:S(2)}) collective-permute-start(bf16[128,1280]{1,0:T(8,128)(2,1)S(1)} %collective-permute-done.15.refs_3_), channel_id=1, source_target_pairs={{0,8},{8,0},{1,9},{9,1},{2,10},{10,2},{3,11},{11,3},{4,12},{12,4},... | collective-permute-start | bytes 983048 | tf_op jit(solution)/shard_map/ppermute | solution.py:278
  247.4 17.6 %collective-permute-start.22 = (bf16[128,1280]{1,0:T(8,128)(2,1)S(1)}, bf16[128,1280]{1,0:T(8,128)(2,1)S(1)}, u32[]{:S(2)}, u32[]{:S(2)}) collective-permute-start(bf16[128,1280]{1,0:T(8,128)(2,1)S(1)} %get-tuple-element.138), channel_id=1, source_target_pairs={{0,1},{1,2},{2,3},{3,0},{4,5},{5,6},{6,7},{7,4},{8,9},{9,10},{10,1... | collective-permute-start | bytes 983048 | tf_op jit(solution)/shard_map/ppermute | solution.py:274
  247.5 17.5 %collective-permute-start.23 = (bf16[128,1280]{1,0:T(8,128)(2,1)S(1)}, bf16[128,1280]{1,0:T(8,128)(2,1)S(1)}, u32[]{:S(2)}, u32[]{:S(2)}) collective-permute-start(bf16[128,1280]{1,0:T(8,128)(2,1)S(1)} %get-tuple-element.140), channel_id=1, source_target_pairs={{0,2},{1,3},{2,0},{3,1},{4,6},{5,7},{6,4},{7,5},{8,10},{9,11},{10,... | collective-permute-start | bytes 983048 | tf_op jit(solution)/shard_map/ppermute | solution.py:274
  249.7 16.4 %collective-permute-start.24 = (bf16[128,1280]{1,0:T(8,128)(2,1)S(1)}, bf16[128,1280]{1,0:T(8,128)(2,1)S(1)}, u32[]{:S(2)}, u32[]{:S(2)}) collective-permute-start(bf16[128,1280]{1,0:T(8,128)(2,1)S(1)} %get-tuple-element.139), channel_id=1, source_target_pairs={{0,3},{1,0},{2,1},{3,2},{4,7},{5,4},{6,5},{7,6},{8,11},{9,8},{10,9... | collective-permute-start | bytes 983048 | tf_op jit(solution)/shard_map/ppermute | solution.py:274
  269.5 16.4 %collective-permute-start.28 = (bf16[128,1280]{1,0:T(8,128)(2,1)S(1)}, bf16[128,1280]{1,0:T(8,128)(2,1)S(1)}, u32[]{:S(2)}, u32[]{:S(2)}) collective-permute-start(bf16[128,1280]{1,0:T(8,128)(2,1)S(1)} %fusion.11.refs_0_), channel_id=1, source_target_pairs={{0,2},{1,3},{2,0},{3,1},{4,6},{5,7},{6,4},{7,5},{8,10},{9,11},{10,... | collective-permute-start | bytes 983048 | tf_op jit(solution)/shard_map/ppermute | solution.py:274
  271.5 15.7 %collective-permute-start.29 = (bf16[128,1280]{1,0:T(8,128)(2,1)S(1)}, bf16[128,1280]{1,0:T(8,128)(2,1)S(1)}, u32[]{:S(2)}, u32[]{:S(2)}) collective-permute-start(bf16[128,1280]{1,0:T(8,128)(2,1)S(1)} %fusion.11.refs_0_), channel_id=1, source_target_pairs={{0,3},{1,0},{2,1},{3,2},{4,7},{5,4},{6,5},{7,6},{8,11},{9,8},{10,9... | collective-permute-start | bytes 983048 | tf_op jit(solution)/shard_map/ppermute | solution.py:274
  310.1 18.5 %collective-permute-start.36 = (bf16[128,1408]{1,0:T(8,128)(2,1)}, bf16[128,1408]{1,0:T(8,128)(2,1)S(1)}, u32[]{:S(2)}, u32[]{:S(2)}) collective-permute-start(bf16[128,1408]{1,0:T(8,128)(2,1)} %get-tuple-element.134), channel_id=1, source_target_pairs={{0,2},{1,3},{2,0},{3,1},{4,6},{5,7},{6,4},{7,5},{8,10},{9,11},{10,... | collective-permute-start | bytes 1081352 | tf_op jit(solution)/shard_map/ppermute | solution.py:274
  312.5 16.3 %collective-permute-start.37 = (bf16[128,1408]{1,0:T(8,128)(2,1)S(1)}, bf16[128,1408]{1,0:T(8,128)(2,1)}, u32[]{:S(2)}, u32[]{:S(2)}) collective-permute-start(bf16[128,1408]{1,0:T(8,128)(2,1)S(1)} %get-tuple-element.133), channel_id=1, source_target_pairs={{0,3},{1,0},{2,1},{3,2},{4,7},{5,4},{6,5},{7,6},{8,11},{9,8},{10,9... | collective-permute-start | bytes 1081352 | tf_op jit(solution)/shard_map/ppermute | solution.py:274
  334.6 17.4 %collective-permute-start.39 = (bf16[128,1280]{1,0:T(8,128)(2,1)S(1)}, bf16[128,1280]{1,0:T(8,128)(2,1)S(1)}, u32[]{:S(2)}, u32[]{:S(2)}) collective-permute-start(bf16[128,1280]{1,0:T(8,128)(2,1)S(1)} %get-tuple-element.128.refs_0_), channel_id=1, source_target_pairs={{0,2},{1,3},{2,0},{3,1},{4,6},{5,7},{6,4},{7,5},{8,10},{9,11},{10,... | collective-permute-start | bytes 983048 | tf_op jit(solution)/shard_map/ppermute | solution.py:274
  337.6 16.8 %collective-permute-start.41 = (bf16[128,1280]{1,0:T(8,128)(2,1)S(1)}, bf16[128,1280]{1,0:T(8,128)(2,1)S(1)}, u32[]{:S(2)}, u32[]{:S(2)}) collective-permute-start(bf16[128,1280]{1,0:T(8,128)(2,1)S(1)} %get-tuple-element.128.refs_0_), channel_id=1, source_target_pairs={{0,8},{8,0},{1,9},{9,1},{2,10},{10,2},{3,11},{11,3},{4,12},{12,4},... | collective-permute-start | bytes 983048 | tf_op jit(solution)/shard_map/ppermute | solution.py:278
  387.6 194.8 %reduce-scatter.9.cloned.1.call-start = ((), (), s32[]{:S(2)}) async-start(), calls=%async_computation.7 | async-start | bytes 4177920
  408.7 17.1 %collective-permute-start.48 = (bf16[128,1280]{1,0:T(8,128)(2,1)S(1)}, bf16[128,1280]{1,0:T(8,128)(2,1)S(1)}, u32[]{:S(2)}, u32[]{:S(2)}) collective-permute-start(bf16[128,1280]{1,0:T(8,128)(2,1)S(1)} %get-tuple-element.137), channel_id=1, source_target_pairs={{0,2},{1,3},{2,0},{3,1},{4,6},{5,7},{6,4},{7,5},{8,10},{9,11},{10,... | collective-permute-start | bytes 983048 | tf_op jit(solution)/shard_map/ppermute | solution.py:274
  411.4 185.8 %collective-permute-start.25 = (bf16[128,1280]{1,0:T(8,128)(2,1)}, bf16[128,1280]{1,0:T(8,128)(2,1)}, u32[]{:S(2)}, u32[]{:S(2)}) collective-permute-start(bf16[128,1280]{1,0:T(8,128)(2,1)} %get-tuple-element.144), channel_id=1, source_target_pairs={{0,0},{4,8},{8,4},{12,12},{1,1},{5,9},{9,5},{13,13},{2,2},{6,10},{... | collective-permute-start | bytes 983048 | tf_op jit(solution)/shard_map/ppermute | solution.py:270
  473.4 119.8 %all-to-all-start.1 = ((bf16[8,10,1152]{2,1,0:T(8,128)(2,1)}), bf16[8,10,1152]{2,1,0:T(8,128)(2,1)}, u32[]{:S(2)}, u32[]{:S(2)}) async-start(bf16[8,10,1152]{2,1,0:T(8,128)(2,1)} %reshape.93), calls=%async_computation.1 | async-start | bytes 589824 | tf_op jit(solution)/shard_map/all_to_all | solution.py:458
  492.1 105.1 %collective-permute-start.50 = (bf16[128,1280]{1,0:T(8,128)(2,1)}, bf16[128,1280]{1,0:T(8,128)(2,1)S(1)}, u32[]{:S(2)}, u32[]{:S(2)}) collective-permute-start(bf16[128,1280]{1,0:T(8,128)(2,1)} %fusion.6), channel_id=1, source_target_pairs={{0,0},{4,8},{8,4},{12,12},{1,1},{5,9},{9,5},{13,13},{2,2},{6,10},{... | collective-permute-start | bytes 983048 | tf_op jit(solution)/shard_map/ppermute | solution.py:270
  (84 other events, 1103.1 us)
Sparse Core Ops, SparseCore 0:
  32.0 86.8 all-gather.2
  121.1 99.5 all-gather.4
  387.7 83.9 reduce-scatter.6
  474.0 108.3 reduce-scatter.8

commit v2 on v1

--- a/solution.py
+++ b/solution.py
@@ -23,6 +23,9 @@
 GU = 4 * 2 * 128
 DN = 4 * 128
 WM = GU + DN
+PART = 80
+SPLIT_A = 640
+SPLIT_M = 768
 norm_eps = 1e-06
 masked_score = -1e30
 rope_base = 10000.0
@@ -43,6 +46,10 @@
     return lax.dot_general(a, b, NT, preferred_element_type=F32)
 
 
+def dot_tn(a, b):
+    return lax.dot_general(a, b, TN, preferred_element_type=F32)
+
+
 def rows_of(start, count=ROWS):
     return pl.ds(pl.multiple_of(start, ROWS), count)
 
@@ -51,11 +58,42 @@
     return pltpu.roll(u, HD // 2, 1)
 
 
+def place_blocks(info, blocks, out, split):
+    for j in range(4):
+        for m in range(4):
+            at = pl.ds(pl.multiple_of(info[32 + j * 4 + m], 16), PART)
+            out[at, :split] = blocks[j][m * PART : (m + 1) * PART, :]
+            out[at, split:] = blocks[4 + m][j * PART : (j + 1) * PART, :]
+
+
+def pick_blocks(info, rows, outs, split):
+    for j in range(4):
+        for m in range(4):
+            at = pl.ds(pl.multiple_of(info[48 + j * 4 + m], 16), PART)
+            outs[j][m * PART : (m + 1) * PART, :] = rows[at, :split]
+            outs[4 + m][j * PART : (j + 1) * PART, :] = rows[at, split:]
+
+
 def attn_fwd_kernel(info, *refs):
     xs = refs[:8]
-    w, cos, sin = refs[8:11]
-    a, b, h1, q, k, v, mixed, lse, ext, chosen = refs[11:21]
-    part, vt = refs[21:]
+    ws = refs[8:16]
+    cos, sin = refs[16:18]
+    a, b, w, h1, q, k, v, mixed, lse, ext, chosen = refs[18:29]
+    part, vt, wp = refs[29:]
+    place_blocks(info, ws, wp, SPLIT_A)
+
+    @pl.loop(0, 8)
+    def _(p):
+        base = pl.multiple_of(p * 2 * PART, 32)
+        low = wp[pl.ds(base, PART), :].astype(F32)
+        high = wp[pl.ds(base + PART, PART), :].astype(F32)
+        half = PART // 2
+        for i in range(2):
+            cut = slice(i * half, (i + 1) * half)
+            w[pl.ds(base + i * PART, PART), :] = jnp.concatenate(
+                [low[cut], high[cut]], axis=0
+            ).astype(BF16)
+
     ext_t = w[:, QKV + HW : WA].astype(F32).T
     ext[...] = ext_t
     gain = ext_t[0:1, :]
@@ -113,9 +151,11 @@
 
 def moe_fwd_kernel(info, *refs):
     hs = refs[:8]
-    w, wm, chosen = refs[8:11]
-    a, b, h2, gu, z, comb = refs[11:17]
-    (part,) = refs[17:]
+    ws = refs[8:16]
+    w, chosen = refs[16:18]
+    a, b, wm, h2, gu, z, comb = refs[18:25]
+    (part,) = refs[25:]
+    place_blocks(info, ws, wm, SPLIT_M)
     for i in range(8):
         h2[rows_of(info[i] * ROWS), :] = hs[i][...]
 
@@ -188,11 +228,23 @@
         b[out, :] = part[rows_of(info[12 + i] * ROWS), :]
 
 
+def moe_grad_kernel(info, *refs):
+    h2, dgu, dm, z = refs[:4]
+    outs = refs[4:12]
+    (rows,) = refs[12:]
+    for i in range(2):
+        cut = slice(i * 640, (i + 1) * 640)
+        rows[cut, :GU] = dot_tn(h2[:, cut], dgu[...]).astype(BF16)
+        rows[cut, GU:] = dot_tn(dm[:, cut], z[...]).astype(BF16)
+    pick_blocks(info, rows, outs, SPLIT_M)
+
+
 def attn_bwd_kernel(info, *refs):
     ds = refs[:8]
-    w, cos, sin, h1, q, k, v, lse, ext = refs[8:17]
-    a, b, da, dqkv, dgain = refs[17:22]
-    part, dmix, kt, dk, dv = refs[22:]
+    w, cos, sin, h1, q, k, v, mixed, lse, sums = refs[8:18]
+    outs = refs[18:26]
+    dqkv = refs[26]
+    da, dmix, kt, dk, dv, rows = refs[27:]
     for i in range(8):
         da[rows_of(info[i] * ROWS), :] = ds[i][...]
 
@@ -235,16 +287,37 @@
         ).astype(BF16)
         dqkv[:, 2 * HW + j * HD : 2 * HW + (j + 1) * HD] = dv[...].astype(BF16)
 
-    dgain[...] = jnp.zeros_like(dgain)
+    half = PART // 2
+    for i in range(2):
+        cut = slice(i * 640, (i + 1) * 640)
+        dw = dot_tn(h1[:, cut], dqkv[...])
+        do = dot_tn(da[:, cut], mixed[...])
+        tail = w[cut, QKV + HW : WA].astype(F32)
+        gain = jnp.sum(dw * w[cut, :QKV].astype(F32), axis=1, keepdims=True) / tail[:, 0:1]
+        extra = sums[:, cut].T
+        lane = lax.broadcasted_iota(jnp.int32, extra.shape, 1)
+        extra = jnp.where(lane == 0, gain, extra)
+        full = jnp.concatenate([dw, do, extra], axis=1)
+        for p in range(4):
+            for g in range(2):
+                top = p * 2 * PART + g * half
+                to = i * 640 + (p * 2 + g) * PART
+                rows[to : to + PART, :] = jnp.concatenate(
+                    [full[top : top + half], full[top + PART : top + PART + half]], axis=0
+                ).astype(BF16)
+    pick_blocks(info, rows, outs, SPLIT_A)
+
+
+def attn_in_kernel(info, *refs):
+    w, dqkv = refs[:2]
+    a, b = refs[2:4]
+    (part,) = refs[4:]
 
     @pl.loop(0, 4)
     def _(step):
         at = rows_of(step * 256, 256)
-        dh = dot_nt(dqkv[at, :], w[:, :QKV])
-        part[at, :] = dh.astype(BF16)
-        dgain[0:1, :] += jnp.sum(dh * h1[at, :].astype(F32), axis=0, keepdims=True)
-
-    dgain[0:1, :] = dgain[0:1, :] / ext[0:1, :]
+        part[at, :] = dot_nt(dqkv[at, :], w[:, :QKV]).astype(BF16)
+
     for i in range(4):
         out = slice(i * ROWS, (i + 1) * ROWS)
         a[out, :] = part[rows_of(info[8 + i] * ROWS), :]
@@ -274,6 +347,37 @@
     return lax.ppermute(x, "z", [(i, (i + k) % 4) for i in range(4)])
 
 
+def along_y(x, k):
+    return lax.ppermute(x, "y", [(i, (i + k) % 4) for i in range(4)])
+
+
+def along_x(x, k):
+    place = [0, 2, 1, 3]
+    return lax.ppermute(x, ("xl", "xh"), [(place[i], place[(i + k) % 4]) for i in range(4)])
+
+
+def gather_plane(x, split):
+    a, b = x[:, :split], x[:, split:]
+    a = jnp.concatenate([a] + [along_x(a, k) for k in (1, 2, 3)], axis=0)
+    b = jnp.concatenate([b] + [along_y(b, k) for k in (1, 2, 3)], axis=0)
+    return [a] + [along_y(a, k) for k in (1, 2, 3)] + [b] + [along_x(b, k) for k in (1, 2, 3)]
+
+
+def add_parts(parts, move):
+    total = parts[0].astype(F32)
+    for k in (1, 2, 3):
+        total = total + move(parts[k], k).astype(F32)
+    return total.astype(BF16)
+
+
+def scatter_plane(blocks):
+    a = add_parts(blocks[:4], along_y)
+    b = add_parts(blocks[4:], along_x)
+    a = add_parts([a[i * PART : (i + 1) * PART] for i in range(4)], along_x)
+    b = add_parts([b[i * PART : (i + 1) * PART] for i in range(4)], along_y)
+    return jnp.concatenate([a, b], axis=1)
+
+
 def to_other_core(x):
     return lax.ppermute(x, "c", [(0, 1), (1, 0)])
 
@@ -315,17 +419,29 @@
     far = [(1 - core) * 4 + (zz + k) % 4 for k in range(4)]
     back = [0, 3, 2, 1]
     sequence = lax.axis_index(PLANE)
+    yy = lax.axis_index("y")
+    xx = lax.axis_index("xh") * 2 + lax.axis_index("xl")
+
+    def place(dy, dx):
+        y, x = (yy + dy) % 4, (xx + dx) % 4
+        return (y * 4 + x % 2 * 2 + x // 2) * PART
+
     info = jnp.stack(
-        [near[i] for i in back] + [far[i] for i in back] + near + far + [prefix[sequence]]
+        [near[i] for i in back]
+        + [far[i] for i in back]
+        + near
+        + far
+        + [prefix[sequence]]
+        + [jnp.int32(0)] * 15
+        + [place(-j, -m) for j in range(4) for m in range(4)]
+        + [place(j, m) for j in range(4) for m in range(4)]
     ).astype(jnp.int32)
 
     lanes = jnp.arange(EXT, dtype=jnp.int32)[None, :]
     chosen = (routes[:, 0:1] + 2 == lanes) | (routes[:, 1:2] + 2 == lanes)
     x_all = exchange(jnp.concatenate([tokens, chosen.astype(BF16)], axis=1))
     small = jnp.concatenate([attn_gain[:, None], ffn_gain[:, None], router_w], axis=1)
-    raw = exchange(
-        jnp.concatenate([w_qkv, w_out, jnp.pad(small, ((0, 0), (0, EXT - 5)))], axis=1)
-    )
+    raw = jnp.concatenate([w_qkv, w_out, jnp.pad(small, ((0, 0), (0, EXT - 5)))], axis=1)
     n = raw.shape[0]
     heads = raw[:, : 4 * D].reshape(n, 4, GROUPS, HW).transpose(2, 0, 1, 3)
     heads = heads.reshape(GROUPS, n, 4 * HW)
@@ -334,7 +450,7 @@
         [heads, jnp.broadcast_to(raw[None, :, 4 * D :], (8, n, EXT))], axis=2
     )
     packed = lax.all_to_all(packed, ("c", "z"), split_axis=0, concat_axis=0)
-    w = lax.all_gather(packed.reshape(8 * n, WA), PLANE, axis=0, tiled=True)
+    w_blocks = gather_plane(packed.reshape(8 * n, WA), SPLIT_A)
     lane_pad = 128 - UNITS
     wm_own = jnp.concatenate(
         [
@@ -343,17 +459,19 @@
         ],
         axis=1,
     )
-    wm = lax.all_gather(exchange(wm_own), PLANE, axis=0, tiled=True)
+    wm_own, _ = lax.optimization_barrier((exchange(wm_own), w_blocks[3]))
+    wm_blocks = gather_plane(wm_own, SPLIT_M)
     teach = exchange(teacher)
     cos, sin = rope_tables()
 
-    (a, b, h1, q, k, v, mixed, lse, ext, chosen_all) = call(
+    (a, b, w, h1, q, k, v, mixed, lse, ext, chosen_all) = call(
         attn_fwd_kernel,
         info,
-        gather_group(x_all) + [w, cos, sin],
+        gather_group(x_all) + w_blocks + [cos, sin],
         [
             ((512, D), BF16),
             ((512, D), BF16),
+            ((D, WA), BF16),
             ((SEQ, D), BF16),
             ((SEQ, HW), BF16),
             ((SEQ, HW), BF16),
@@ -363,7 +481,7 @@
             ((EXT, D), F32),
             ((SEQ, EXT), BF16),
         ],
-        [((SEQ, D), BF16), ((HW, SEQ), BF16)],
+        [((SEQ, D), BF16), ((HW, SEQ), BF16), ((D, WA), BF16)],
         4_000_000_000,
     )
     x = x_all[:, :D].astype(F32)
@@ -373,13 +491,14 @@
     gain_two = ext[1:2, :]
     h2 = (n2 * gain_two).astype(BF16)
 
-    a, b, h2_all, gu, z, comb = call(
+    a, b, wm, h2_all, gu, z, comb = call(
         moe_fwd_kernel,
         info,
-        gather_group(h2) + [w, wm, chosen_all],
+        gather_group(h2) + wm_blocks + [w, chosen_all],
         [
             ((512, D), BF16),
             ((512, D), BF16),
+            ((D, WM), BF16),
             ((SEQ, D), BF16),
             ((SEQ, GU), F32),
             ((SEQ, DN), BF16),
@@ -400,14 +519,15 @@
         [((SEQ, D + EXT), BF16)],
         4_000_000_000,
     )
-    dwm = jnp.concatenate(
-        [
-            lax.dot_general(h2_all, dgu, TN, preferred_element_type=F32).astype(BF16),
-            lax.dot_general(dm_all, z, TN, preferred_element_type=F32).astype(BF16),
-        ],
-        axis=1,
-    )
-    dwm_own = exchange(lax.psum_scatter(dwm, PLANE, scatter_dimension=0, tiled=True))
+    dwm_blocks = call(
+        moe_grad_kernel,
+        info,
+        [h2_all, dgu, dm_all, z],
+        [((4 * PART, SPLIT_M), BF16)] * 4 + [((4 * PART, WM - SPLIT_M), BF16)] * 4,
+        [((D, WM), BF16)],
+        4_000_000_000,
+    )
+    dwm_own = exchange(scatter_plane(dwm_blocks))
     dh2 = scatter_group(a, b)
     dcomb = dh2[:, D + 2 : D + 5] + dh2[:, D + 5 : D + 8]
     router = ext[2:5, :].astype(BF16)
@@ -422,45 +542,48 @@
     dx1 = diff + r2 * (g2 - n2 * jnp.mean(g2 * n2, axis=1, keepdims=True))
     da = dx1.astype(BF16)
 
-    a, b, da_all, dqkv, dgain = call(
+    sums = jnp.concatenate(
+        [
+            jnp.zeros((1, D), F32),
+            d_ffn_gain,
+            d_router,
+            jnp.full((1, D), squares / (SEQ * 16), F32),
+        ],
+        axis=0,
+    )
+    sums = jnp.pad(sums, ((0, EXT - 6), (0, 0)))
+    *dw_blocks, dqkv = call(
         attn_bwd_kernel,
         info,
-        gather_group(da) + [w, cos, sin, h1, q, k, v, lse, ext],
-        [
-            ((512, D), BF16),
-            ((512, D), BF16),
-            ((SEQ, D), BF16),
-            ((SEQ, QKV), BF16),
-            ((8, D), F32),
-        ],
+        gather_group(da) + [w, cos, sin, h1, q, k, v, mixed, lse, sums],
+        [((4 * PART, SPLIT_A), BF16)] * 4
+        + [((4 * PART, WA - SPLIT_A), BF16)] * 4
+        + [((SEQ, QKV), BF16)],
         [
             ((SEQ, D), BF16),
             ((SEQ, HW), BF16),
             ((HW, SEQ), BF16),
             ((SEQ, HD), F32),
             ((SEQ, HD), F32),
+            ((D, WA), BF16),
         ],
         6_000_000_000,
     )
-    sums = jnp.concatenate(
-        [dgain[0:1], d_ffn_gain, d_router, jnp.full((1, D), squares / (SEQ * 16), F32)], axis=0
-    )
-    sums = jnp.pad(sums, ((0, EXT - 6), (0, 0))).T
-    dw = jnp.concatenate(
-        [
-            lax.dot_general(h1, dqkv, TN, preferred_element_type=F32).astype(BF16),
-            lax.dot_general(da_all, mixed, TN, preferred_element_type=F32).astype(BF16),
-            sums.astype(BF16),
-        ],
-        axis=1,
-    )
-    dw = lax.psum_scatter(dw, PLANE, scatter_dimension=0, tiled=True)
+    a, b = call(
+        attn_in_kernel,
+        info,
+        [w, dqkv],
+        [((512, D), BF16), ((512, D), BF16)],
+        [((SEQ, D), BF16)],
+        2_000_000_000,
+    )
+    dw = scatter_plane(dw_blocks)
     dw = lax.all_to_all(dw.reshape(8, n, WA), ("c", "z"), split_axis=0, concat_axis=0)
     dw_heads = dw[:GROUPS, :, : 4 * HW].reshape(GROUPS, n, 4, HW).transpose(1, 2, 0, 3)
     dw_small = jnp.sum(dw[:, :, 4 * HW :].astype(F32), axis=0)
-    d_raw = exchange(
-        jnp.concatenate([dw_heads.reshape(n, 4 * D), dw_small.astype(BF16)], axis=1)
-    ).astype(F32)
+    d_raw = jnp.concatenate(
+        [dw_heads.reshape(n, 4 * D).astype(F32), dw_small], axis=1
+    )
 
     dh1 = scatter_group(a, b)
     r1 = lax.rsqrt(jnp.mean(x * x, axis=1, keepdims=True) + norm_eps)

time: 627 us -> 456 us (0.73)
  waiting for transfers between devices: 332 us -> 116 us
  starting transfers between devices: 115 us -> 190 us
  Pallas kernels: 70.4 us -> 89.4 us
  local copies, waits for them, and re-layouts: 31.3 us -> 16.8 us
  between operations: 15.8 us -> 2.94 us
  blocking collectives: 12.6 us -> 0 us
  matrix products: 13.2 us -> 3.65 us
    unnamed x5 -> x0, waiting for transfers between devices: 88.4 us -> none
    all_gather x2 -> x0, waiting for transfers between devices: 78.6 us -> none  [the longest x1 47.3 us: on_device(): w = lax.all_gather(packed.reshape(8 * n, WA), PLANE, axis=0, tiled=True)]
    ppermute x0 -> x48, starting transfers between devices: none -> 73.5 us  [the longest x24 37.3 us: along_x(): lax.ppermute(x, ('xl', 'xh'), [(place[i], place[(i + k) % 4]) for i in ra...]
    ppermute x0 -> x48, waiting for transfers between devices: none -> 60.2 us  [the longest x24 31.8 us: along_y(): return lax.ppermute(x, 'y', [(i, (i + k) % 4) for i in range(4)])]
    ppermute x24, waiting for transfers between devices: 90.9 us -> 37.6 us  [along_z(): return lax.ppermute(x, 'z', [(i, (i + k) % 4) for i in range(4)])]
    reduce_scatter x1 -> x0, waiting for transfers between devices: 45 us -> none  [on_device(): dw = lax.psum_scatter(dw, PLANE, scatter_dimension=0, tiled=True)]
    pallas_call x4 -> x6, Pallas kernels: 70.4 us -> 89.4 us  [call(): pl.pallas_call(kernel, out_shape=[jax.ShapeDtypeStruct(s, t) for s, t in...]
    unnamed x111 -> x154, local copies, waits for them, and re-layouts: 20.6 us -> 5.87 us
  transfers between devices with their start and end apart: 57 -> 100, of which waited for: 35 -> 33; matrix products, arithmetic and copies ran while one was open for 6% -> 8% of each run, Pallas kernels for 3% -> 7%
where the time goes in v2:
time: 456 us; the launch traced here: 449 us
  starting transfers between devices  190 us (42%)
  waiting for transfers between devices  116 us (25%)
  Pallas kernels  89.4 us (20%)
  other arithmetic  30.8 us (7%)
  local copies, waits for them, and re-layouts  16.8 us (4%)
    pallas_call x6, Pallas kernels, call(): pl.pallas_call(kernel, out_shape=[jax.ShapeDtypeStruct(s, t) for s, t in...  89.4 us
    ppermute x24, starting transfers between devices, along_z(): return lax.ppermute(x, 'z', [(i, (i + k) % 4) for i in range(4)])  40.5 us
    ppermute x24, waiting for transfers between devices, along_z(): return lax.ppermute(x, 'z', [(i, (i + k) % 4) for i in range(4)])  37.6 us
    ppermute x24, starting transfers between devices, along_x(): lax.ppermute(x, ('xl', 'xh'), [(place[i], place[(i + k) % 4]) for i in ra...  37.3 us
    ppermute x24, starting transfers between devices, along_y(): return lax.ppermute(x, 'y', [(i, (i + k) % 4) for i in range(4)])  36.2 us
    ppermute x6, starting transfers between devices, exchange(): return lax.ppermute(x, ('c', 'xh'), [(0, 0), (1, 2), (2, 1), (3, 3)])  32 us
    ppermute x24, waiting for transfers between devices, along_y(): return lax.ppermute(x, 'y', [(i, (i + k) % 4) for i in range(4)])  31.8 us
    ppermute x20, starting transfers between devices, to_other_core(): return lax.ppermute(x, 'c', [(0, 1), (1, 0)])  30.1 us
  transfers between devices with their start and end apart: 100, of which 33 were waited for; matrix products, arithmetic and copies ran while one was open for 8% of the time, Pallas kernels for 7%

profile of v2, /device:TPU:1, one launch (start us, length us, event | category | flops | bytes accessed | tf_op | source)
XLA Modules:
  0.0 449.3 jit_solution(11536858590804218706)
XLA Ops:
  3.5 6.8 %all-to-all-start = ((bf16[8,10,1152]{2,1,0:T(8,128)(2,1)}), bf16[8,10,1152]{2,1,0:T(8,128)(2,1)S(1)}, u32[]{:S(2)}, u32[]{:S(2)}) async-start(bf16[8,10,1152]{2,1,0:T(8,128)(2,1)} %fusion.9), calls=%async_computation | async-start | bytes 589824 | tf_op jit(solution)/shard_map/all_to_all | solution.py:452
  10.4 6.8 %all-to-all-done = bf16[8,10,1152]{2,1,0:T(8,128)(2,1)S(1)} async-done(((bf16[8,10,1152]{2,1,0:T(8,128)(2,1)}), bf16[8,10,1152]{2,1,0:T(8,128)(2,1)S(1)}, u32[]{:S(2)}, u32[]{:S(2)}) %all-to-all-start) | async-done | bytes 184352 | tf_op jit(solution)/shard_map/all_to_all | solution.py:452
  22.4 5.7 %collective-permute-start = (bf16[128,1408]{1,0:T(8,128)(2,1)S(1)}, bf16[128,1408]{1,0:T(8,128)(2,1)S(1)}, u32[]{:S(2)}, u32[]{:S(2)}) collective-permute-start(bf16[128,1408]{1,0:T(8,128)(2,1)S(1)} %pad_maximum_fusion.5), channel_id=1, source_target_pairs={{0,0},{4,8},{8,4},{12,12},{1,1},{5,9},{9,5},{13,13},{2,2},{6,10},{... | collective-permute-start | bytes 1081352 | tf_op jit(solution)/shard_map/ppermute | solution.py:343
  32.3 9.2 %collective-permute-done.10 = bf16[80,640]{1,0:T(8,128)(2,1)S(1)} collective-permute-done((bf16[80,640]{1,0:T(8,128)(2,1)S(1)}, bf16[80,640]{1,0:T(8,128)(2,1)S(1)}, u32[]{:S(2)}, u32[]{:S(2)}) %collective-permute-start.10) | collective-permute-done | bytes 102432 | tf_op jit(solution)/shard_map/ppermute | solution.py:356
  45.1 6.2 %collective-permute-done.9 = bf16[80,640]{1,0:T(8,128)(2,1)S(1)} collective-permute-done((bf16[80,640]{1,0:T(8,128)(2,1)S(1)}, bf16[80,640]{1,0:T(8,128)(2,1)S(1)}, u32[]{:S(2)}, u32[]{:S(2)}) %collective-permute-start.9) | collective-permute-done | bytes 102432 | tf_op jit(solution)/shard_map/ppermute | solution.py:356
  78.1 21.4 %shard_map.186 = (bf16[512,1280]{1,0:T(8,128)(2,1)}, bf16[512,1280]{1,0:T(8,128)(2,1)}, bf16[1280,1152]{1,0:T(8,128)(2,1)}, bf16[1024,1280]{1,0:T(8,128)(2,1)}, ...) custom-call(s32[64]{0:T(128)} %stack.168.info, ...), custom_call_target="tpu_custom_call" | custom-call | flops 4000000000 | bytes 18120704 | tf_op jit(solution)/shard_map/pallas_call | solution.py:330
  105.0 5.3 %collective-permute-done.31 = bf16[80,1536]{1,0:T(8,128)(2,1)S(1)} collective-permute-done((bf16[80,1536]{1,0:T(8,128)(2,1)S(1)}, bf16[80,1536]{1,0:T(8,128)(2,1)S(1)}, u32[]{:S(2)}, u32[]{:S(2)}) %collective-permute-start.31) | collective-permute-done | bytes 245792 | tf_op jit(solution)/shard_map/ppermute | solution.py:343
  129.9 7.3 %collective-permute-done.22 = bf16[128,1280]{1,0:T(8,128)(2,1)S(1)} collective-permute-done((bf16[128,1280]{1,0:T(8,128)(2,1)S(1)}, bf16[128,1280]{1,0:T(8,128)(2,1)S(1)}, u32[]{:S(2)}, u32[]{:S(2)}) %collective-permute-start.22) | collective-permute-done | bytes 327712 | tf_op jit(solution)/shard_map/ppermute | solution.py:347
  153.6 7.7 %collective-permute-done.42.refs_14_ = bf16[320,768]{1,0:T(8,128)(2,1)S(1)} collective-permute-done((bf16[320,768]{1,0:T(8,128)(2,1)S(1)}, bf16[320,768]{1,0:T(8,128)(2,1)S(1)}, u32[]{:S(2)}, u32[]{:S(2)}) %collective-permute-start.42) | collective-permute-done | bytes 491552 | tf_op jit(solution)/shard_map/ppermute | solution.py:356
  166.8 16.0 %shard_map.187 = (bf16[512,1280]{1,0:T(8,128)(2,1)}, bf16[512,1280]{1,0:T(8,128)(2,1)}, bf16[1280,1536]{1,0:T(8,128)(2,1)}, bf16[1024,1280]{1,0:T(8,128)(2,1)}, ...) custom-call(s32[64]{0:T(128)} %stack.168.info, bf16[128,1280]{1,0:T(8,128)(2,1)} %copy-done.2, ...), custom_call_target="tpu_custom_call" | custom-call | flops 4000000000 | bytes 24707072 | tf_op jit(solution)/shard_map/pallas_call | solution.py:330
  201.5 5.2 %collective-permute-done.46 = bf16[128,1280]{1,0:T(8,128)(2,1)S(1)} collective-permute-done((bf16[128,1280]{1,0:T(8,128)(2,1)S(1)}, bf16[128,1280]{1,0:T(8,128)(2,1)S(1)}, u32[]{:S(2)}, u32[]{:S(2)}) %collective-permute-start.46) | collective-permute-done | bytes 327712 | tf_op jit(solution)/shard_map/ppermute | solution.py:347
  220.3 6.8 %collective-permute-done.51.refs_2_ = bf16[128,1280]{1,0:T(8,128)(2,1)S(1)} collective-permute-done((bf16[128,1280]{1,0:T(8,128)(2,1)S(1)}, bf16[128,1280]{1,0:T(8,128)(2,1)S(1)}, u32[]{:S(2)}, u32[]{:S(2)}) %collective-permute-start.51) | collective-permute-done | bytes 327712 | tf_op jit(solution)/shard_map/ppermute | solution.py:347
  230.9 13.1 %shard_map.188 = (bf16[512,1408]{1,0:T(8,128)(2,1)}, bf16[512,1408]{1,0:T(8,128)(2,1)}, bf16[1024,1280]{1,0:T(8,128)(2,1)}, bf16[1024,1024]{1,0:T(8,128)(2,1)}) custom-call(s32[64]{0:T(128)} %stack.168.info, bf16[128,1280]{1,0:T(8,128)(2,1)} %copy-done.15, bf16[128,1280]{1,0:T(8,128)(2,1)} %copy-done.63, bf16[128,1280]{1,0:T(8,128)(2,1)} %copy-done.64, ...), custom_call_target="tpu_custom_call" | custom-call | flops 4000000000 | bytes 18874368 | tf_op jit(solution)/shard_map/pallas_call | solution.py:330
  244.0 9.6 %shard_map.191 = (bf16[320,768]{1,0:T(8,128)(2,1)}, bf16[320,768]{1,0:T(8,128)(2,1)}, bf16[320,768]{1,0:T(8,128)(2,1)}, bf16[320,768]{1,0:T(8,128)(2,1)}, bf16[3...) custom-call(s32[64]{0:T(128)} %stack.168.info, ...), custom_call_target="tpu_custom_call" | custom-call | flops 4000000000 | bytes 12320768 | tf_op jit(solution)/shard_map/pallas_call | solution.py:330
  262.6 5.2 %collective-permute-done.85 = bf16[320,768]{1,0:T(8,128)(2,1)S(1)} collective-permute-done((bf16[320,768]{1,0:T(8,128)(2,1)}, bf16[320,768]{1,0:T(8,128)(2,1)S(1)}, u32[]{:S(2)}, u32[]{:S(2)}) %collective-permute-start.85) | collective-permute-done | bytes 491552 | tf_op jit(solution)/shard_map/ppermute | solution.py:351
  271.5 7.9 %collective-permute-done.86 = bf16[320,768]{1,0:T(8,128)(2,1)S(1)} collective-permute-done((bf16[320,768]{1,0:T(8,128)(2,1)}, bf16[320,768]{1,0:T(8,128)(2,1)S(1)}, u32[]{:S(2)}, u32[]{:S(2)}) %collective-permute-start.86) | collective-permute-done | bytes 491552 | tf_op jit(solution)/shard_map/ppermute | solution.py:351
  305.9 8.2 %collective-permute-start.97 = (bf16[80,1536]{1,0:T(8,128)(2,1)}, bf16[80,1536]{1,0:T(8,128)(2,1)S(1)}, u32[]{:S(2)}, u32[]{:S(2)}) collective-permute-start(bf16[80,1536]{1,0:T(8,128)(2,1)} %pad_maximum_fusion.8), channel_id=1, source_target_pairs={{0,0},{4,8},{8,4},{12,12},{1,1},{5,9},{9,5},{13,13},{2,2},{6,10},{... | collective-permute-start | bytes 737288 | tf_op jit(solution)/shard_map/ppermute | solution.py:343
  334.8 7.7 %collective-permute-start.65 = (bf16[128,1280]{1,0:T(8,128)(2,1)S(1)}, bf16[128,1280]{1,0:T(8,128)(2,1)S(1)}, u32[]{:S(2)}, u32[]{:S(2)}) collective-permute-start(bf16[128,1280]{1,0:T(8,128)(2,1)S(1)} %collective-permute-done.61.refs_1_), channel_id=1, source_target_pairs={{0,8},{8,0},{1,9},{9,1},{2,10},{10,2},{3,11},{11,3},{4,12},{12,4},... | collective-permute-start | bytes 983048 | tf_op jit(solution)/shard_map/ppermute | solution.py:382
  347.8 22.3 %shard_map.189 = (bf16[320,640]{1,0:T(8,128)(2,1)}, bf16[320,640]{1,0:T(8,128)(2,1)}, bf16[320,640]{1,0:T(8,128)(2,1)}, bf16[320,640]{1,0:T(8,128)(2,1)}, bf16[3...) custom-call(s32[64]{0:T(128)} %stack.168.info, ...), custom_call_target="tpu_custom_call" | custom-call | flops 6000000000 | bytes 16547840 | tf_op jit(solution)/shard_map/pallas_call | solution.py:330
  375.2 7.0 %shard_map.190 = (bf16[512,1280]{1,0:T(8,128)(2,1)}, bf16[512,1280]{1,0:T(8,128)(2,1)}) custom-call(s32[64]{0:T(128)} %stack.168.info, bf16[1280,1152]{1,0:T(8,128)(2,1)} %get-tuple-element.56.refs_16_.refs_8_.refs_0_, bf16[1024,768]{1,0:T(8,128)(2,1)} %get-tuple-element.79.refs_1_), custom_call_target="tpu_custom_call" | custom-call | flops 2000000000 | bytes 7143424 | tf_op jit(solution)/shard_map/pallas_call | solution.py:330
  385.2 6.6 %collective-permute-start.69 = (bf16[320,640]{1,0:T(8,128)(2,1)S(1)}, bf16[320,640]{1,0:T(8,128)(2,1)S(1)}, u32[]{:S(2)}, u32[]{:S(2)}) collective-permute-start(bf16[320,640]{1,0:T(8,128)(2,1)S(1)} %copy-done.40), channel_id=1, source_target_pairs={{0,64},{32,96},{64,0},{96,32},{1,65},{33,97},{65,1},{97,33},{2,66}... | collective-permute-start | bytes 1228808 | tf_op jit(solution)/shard_map/ppermute | solution.py:351
  396.7 11.8 %collective-permute-start.78 = (bf16[80,512]{1,0:T(8,128)(2,1)S(1)}, bf16[80,512]{1,0:T(8,128)(2,1)S(1)}, u32[]{:S(2)}, u32[]{:S(2)}) collective-permute-start(bf16[80,512]{1,0:T(8,128)(2,1)S(1)} %get-tuple-element.161), channel_id=1, source_target_pairs={{0,64},{32,96},{64,0},{96,32},{1,65},{33,97},{65,1},{97,33},{2,66}... | collective-permute-start | bytes 245768 | tf_op jit(solution)/shard_map/ppermute | solution.py:351
  420.9 6.9 %all-to-all-start.1 = ((bf16[8,10,1152]{2,1,0:T(8,128)(2,1)}), bf16[8,10,1152]{2,1,0:T(8,128)(2,1)}, u32[]{:S(2)}, u32[]{:S(2)}) async-start(bf16[8,10,1152]{2,1,0:T(8,128)(2,1)} %reshape.93), calls=%async_computation.1 | async-start | bytes 589824 | tf_op jit(solution)/shard_map/all_to_all | solution.py:581
  434.5 7.3 %collective-permute-start.84 = (bf16[128,1280]{1,0:T(8,128)(2,1)}, bf16[128,1280]{1,0:T(8,128)(2,1)S(1)}, u32[]{:S(2)}, u32[]{:S(2)}) collective-permute-start(bf16[128,1280]{1,0:T(8,128)(2,1)} %fusion.6), channel_id=1, source_target_pairs={{0,0},{4,8},{8,4},{12,12},{1,1},{5,9},{9,5},{13,13},{2,2},{6,10},{... | collective-permute-start | bytes 983048 | tf_op jit(solution)/shard_map/ppermute | solution.py:343
  (430 shorter events, 228.3 us)
Async XLA Ops:
  22.4 29.0 %collective-permute-start = (bf16[128,1408]{1,0:T(8,128)(2,1)S(1)}, bf16[128,1408]{1,0:T(8,128)(2,1)S(1)}, u32[]{:S(2)}, u32[]{:S(2)}) collective-permute-start(bf16[128,1408]{1,0:T(8,128)(2,1)S(1)} %pad_maximum_fusion.5), channel_id=1, source_target_pairs={{0,0},{4,8},{8,4},{12,12},{1,1},{5,9},{9,5},{13,13},{2,2},{6,10},{... | collective-permute-start | bytes 1081352 | tf_op jit(solution)/shard_map/ppermute | solution.py:343
  29.7 23.1 %collective-permute-start.17 = (bf16[320,512]{1,0:T(8,128)(2,1)S(1)}, bf16[320,512]{1,0:T(8,128)(2,1)S(1)}, u32[]{:S(2)}, u32[]{:S(2)}) collective-permute-start(bf16[320,512]{1,0:T(8,128)(2,1)S(1)} %pad_maximum_fusion.6.refs_12_), channel_id=1, source_target_pairs={{0,16},{16,4},{4,20},{20,0},{1,17},{17,5},{5,21},{21,1},{2,18},{18... | collective-permute-start | bytes 983048 | tf_op jit(solution)/shard_map/ppermute | solution.py:356
  30.1 23.3 %collective-permute-start.18 = (bf16[320,512]{1,0:T(8,128)(2,1)S(1)}, bf16[320,512]{1,0:T(8,128)(2,1)S(1)}, u32[]{:S(2)}, u32[]{:S(2)}) collective-permute-start(bf16[320,512]{1,0:T(8,128)(2,1)S(1)} %pad_maximum_fusion.6.refs_12_), channel_id=1, source_target_pairs={{0,4},{16,20},{4,0},{20,16},{1,5},{17,21},{5,1},{21,17},{2,6},{18,... | collective-permute-start | bytes 983048 | tf_op jit(solution)/shard_map/ppermute | solution.py:356
  55.6 17.1 %collective-permute-start.3 = (bf16[128,1408]{1,0:T(8,128)(2,1)S(1)}, bf16[128,1408]{1,0:T(8,128)(2,1)S(1)}, u32[]{:S(2)}, u32[]{:S(2)}) collective-permute-start(bf16[128,1408]{1,0:T(8,128)(2,1)S(1)} %collective-permute-done.refs_0_), channel_id=1, source_target_pairs={{0,3},{1,0},{2,1},{3,2},{4,7},{5,4},{6,5},{7,6},{8,11},{9,8},{10,9... | collective-permute-start | bytes 1081352 | tf_op jit(solution)/shard_map/ppermute | solution.py:347
  124.6 17.6 %collective-permute-start.35 = (bf16[320,768]{1,0:T(8,128)(2,1)S(1)}, bf16[320,768]{1,0:T(8,128)(2,1)S(1)}, u32[]{:S(2)}, u32[]{:S(2)}) collective-permute-start(bf16[320,768]{1,0:T(8,128)(2,1)S(1)} %pad_maximum_fusion.2.refs_8_), channel_id=1, source_target_pairs={{0,32},{32,64},{64,96},{96,0},{1,33},{33,65},{65,97},{97,1},{2,34}... | collective-permute-start | bytes 1474568 | tf_op jit(solution)/shard_map/ppermute | solution.py:351
  125.2 20.6 %collective-permute-start.36 = (bf16[320,768]{1,0:T(8,128)(2,1)S(1)}, bf16[320,768]{1,0:T(8,128)(2,1)S(1)}, u32[]{:S(2)}, u32[]{:S(2)}) collective-permute-start(bf16[320,768]{1,0:T(8,128)(2,1)S(1)} %pad_maximum_fusion.2.refs_8_), channel_id=1, source_target_pairs={{0,64},{32,96},{64,0},{96,32},{1,65},{33,97},{65,1},{97,33},{2,66}... | collective-permute-start | bytes 1474568 | tf_op jit(solution)/shard_map/ppermute | solution.py:351
  129.5 20.0 %collective-permute-start.37 = (bf16[320,768]{1,0:T(8,128)(2,1)S(1)}, bf16[320,768]{1,0:T(8,128)(2,1)S(1)}, u32[]{:S(2)}, u32[]{:S(2)}) collective-permute-start(bf16[320,768]{1,0:T(8,128)(2,1)S(1)} %pad_maximum_fusion.2.refs_8_), channel_id=1, source_target_pairs={{0,96},{32,0},{64,32},{96,64},{1,97},{33,1},{65,33},{97,65},{2,98}... | collective-permute-start | bytes 1474568 | tf_op jit(solution)/shard_map/ppermute | solution.py:351
  137.7 23.6 %collective-permute-start.42 = (bf16[320,768]{1,0:T(8,128)(2,1)S(1)}, bf16[320,768]{1,0:T(8,128)(2,1)S(1)}, u32[]{:S(2)}, u32[]{:S(2)}) collective-permute-start(bf16[320,768]{1,0:T(8,128)(2,1)S(1)} %pad_maximum_fusion.3.refs_12_), channel_id=1, source_target_pairs={{0,4},{16,20},{4,0},{20,16},{1,5},{17,21},{5,1},{21,17},{2,6},{18,... | collective-permute-start | bytes 1474568 | tf_op jit(solution)/shard_map/ppermute | solution.py:356
  142.2 21.1 %collective-permute-start.24 = (bf16[128,1280]{1,0:T(8,128)(2,1)S(1)}, bf16[128,1280]{1,0:T(8,128)(2,1)S(1)}, u32[]{:S(2)}, u32[]{:S(2)}) collective-permute-start(bf16[128,1280]{1,0:T(8,128)(2,1)S(1)} %multiply_convert_fusion.refs_0_), channel_id=1, source_target_pairs={{0,1},{1,2},{2,3},{3,0},{4,5},{5,6},{6,7},{7,4},{8,9},{9,10},{10,1... | collective-permute-start | bytes 983048 | tf_op jit(solution)/shard_map/ppermute | solution.py:347
  145.8 17.7 %collective-permute-start.25 = (bf16[128,1280]{1,0:T(8,128)(2,1)S(1)}, bf16[128,1280]{1,0:T(8,128)(2,1)S(1)}, u32[]{:S(2)}, u32[]{:S(2)}) collective-permute-start(bf16[128,1280]{1,0:T(8,128)(2,1)S(1)} %multiply_convert_fusion.refs_0_), channel_id=1, source_target_pairs={{0,2},{1,3},{2,0},{3,1},{4,6},{5,7},{6,4},{7,5},{8,10},{9,11},{10,... | collective-permute-start | bytes 983048 | tf_op jit(solution)/shard_map/ppermute | solution.py:347
  253.6 25.7 %collective-permute-start.86 = (bf16[320,768]{1,0:T(8,128)(2,1)}, bf16[320,768]{1,0:T(8,128)(2,1)S(1)}, u32[]{:S(2)}, u32[]{:S(2)}) collective-permute-start(bf16[320,768]{1,0:T(8,128)(2,1)} %get-tuple-element.88), channel_id=1, source_target_pairs={{0,64},{32,96},{64,0},{96,32},{1,65},{33,97},{65,1},{97,33},{2,66}... | collective-permute-start | bytes 1474568 | tf_op jit(solution)/shard_map/ppermute | solution.py:351
  257.6 25.1 %collective-permute-start.87 = (bf16[320,768]{1,0:T(8,128)(2,1)}, bf16[320,768]{1,0:T(8,128)(2,1)}, u32[]{:S(2)}, u32[]{:S(2)}) collective-permute-start(bf16[320,768]{1,0:T(8,128)(2,1)} %get-tuple-element.89), channel_id=1, source_target_pairs={{0,96},{32,0},{64,32},{96,64},{1,97},{33,1},{65,33},{97,65},{2,98}... | collective-permute-start | bytes 1474568 | tf_op jit(solution)/shard_map/ppermute | solution.py:351
  259.3 25.3 %collective-permute-start.91 = (bf16[320,768]{1,0:T(8,128)(2,1)}, bf16[320,768]{1,0:T(8,128)(2,1)S(1)}, u32[]{:S(2)}, u32[]{:S(2)}) collective-permute-start(bf16[320,768]{1,0:T(8,128)(2,1)} %get-tuple-element.91), channel_id=1, source_target_pairs={{0,16},{16,4},{4,20},{20,0},{1,17},{17,5},{5,21},{21,1},{2,18},{18... | collective-permute-start | bytes 1474568 | tf_op jit(solution)/shard_map/ppermute | solution.py:356
  260.4 25.1 %collective-permute-start.92 = (bf16[320,768]{1,0:T(8,128)(2,1)}, bf16[320,768]{1,0:T(8,128)(2,1)S(1)}, u32[]{:S(2)}, u32[]{:S(2)}) collective-permute-start(bf16[320,768]{1,0:T(8,128)(2,1)} %get-tuple-element.92), channel_id=1, source_target_pairs={{0,4},{16,20},{4,0},{20,16},{1,5},{17,21},{5,1},{21,17},{2,6},{18,... | collective-permute-start | bytes 1474568 | tf_op jit(solution)/shard_map/ppermute | solution.py:356
  267.8 19.7 %collective-permute-start.93 = (bf16[320,768]{1,0:T(8,128)(2,1)}, bf16[320,768]{1,0:T(8,128)(2,1)S(1)}, u32[]{:S(2)}, u32[]{:S(2)}) collective-permute-start(bf16[320,768]{1,0:T(8,128)(2,1)} %get-tuple-element.93), channel_id=1, source_target_pairs={{0,20},{16,0},{4,16},{20,4},{1,21},{17,1},{5,17},{21,5},{2,22},{18... | collective-permute-start | bytes 1474568 | tf_op jit(solution)/shard_map/ppermute | solution.py:356
  279.4 18.8 %collective-permute-start.57 = (bf16[512,1408]{1,0:T(8,128)(2,1)}, bf16[512,1408]{1,0:T(8,128)(2,1)S(1)}, u32[]{:S(2)}, u32[]{:S(2)}) collective-permute-start(bf16[512,1408]{1,0:T(8,128)(2,1)} %get-tuple-element.64), channel_id=1, source_target_pairs={{0,8},{8,0},{1,9},{9,1},{2,10},{10,2},{3,11},{11,3},{4,12},{12,4},... | collective-permute-start | bytes 4325384 | tf_op jit(solution)/shard_map/ppermute | solution.py:382
  299.7 18.8 %collective-permute-start.58 = (bf16[128,1408]{1,0:T(8,128)(2,1)}, bf16[128,1408]{1,0:T(8,128)(2,1)S(1)}, u32[]{:S(2)}, u32[]{:S(2)}) collective-permute-start(bf16[128,1408]{1,0:T(8,128)(2,1)} %get-tuple-element.136), channel_id=1, source_target_pairs={{0,1},{1,2},{2,3},{3,0},{4,5},{5,6},{6,7},{7,4},{8,9},{9,10},{10,1... | collective-permute-start | bytes 1081352 | tf_op jit(solution)/shard_map/ppermute | solution.py:347
  329.0 17.7 %collective-permute-start.64 = (bf16[128,1280]{1,0:T(8,128)(2,1)}, bf16[128,1280]{1,0:T(8,128)(2,1)S(1)}, u32[]{:S(2)}, u32[]{:S(2)}) collective-permute-start(bf16[128,1280]{1,0:T(8,128)(2,1)} %get-tuple-element.132.refs_0_), channel_id=1, source_target_pairs={{0,8},{8,0},{1,9},{9,1},{2,10},{10,2},{3,11},{11,3},{4,12},{12,4},... | collective-permute-start | bytes 983048 | tf_op jit(solution)/shard_map/ppermute | solution.py:382
  344.8 39.5 %collective-permute-start.48 = (bf16[128,1280]{1,0:T(8,128)(2,1)S(1)}, bf16[128,1280]{1,0:T(8,128)(2,1)S(1)}, u32[]{:S(2)}, u32[]{:S(2)}) collective-permute-start(bf16[128,1280]{1,0:T(8,128)(2,1)S(1)} %get-tuple-element.148), channel_id=1, source_target_pairs={{0,0},{4,8},{8,4},{12,12},{1,1},{5,9},{9,5},{13,13},{2,2},{6,10},{... | collective-permute-start | bytes 983048 | tf_op jit(solution)/shard_map/ppermute | solution.py:343
  372.7 19.0 %collective-permute-start.75 = (bf16[320,512]{1,0:T(8,128)(2,1)}, bf16[320,512]{1,0:T(8,128)(2,1)S(1)}, u32[]{:S(2)}, u32[]{:S(2)}) collective-permute-start(bf16[320,512]{1,0:T(8,128)(2,1)} %get-tuple-element.77), channel_id=1, source_target_pairs={{0,4},{16,20},{4,0},{20,16},{1,5},{17,21},{5,1},{21,17},{2,6},{18,... | collective-permute-start | bytes 983048 | tf_op jit(solution)/shard_map/ppermute | solution.py:356
  372.8 19.1 %collective-permute-start.76 = (bf16[320,512]{1,0:T(8,128)(2,1)}, bf16[320,512]{1,0:T(8,128)(2,1)S(1)}, u32[]{:S(2)}, u32[]{:S(2)}) collective-permute-start(bf16[320,512]{1,0:T(8,128)(2,1)} %get-tuple-element.78), channel_id=1, source_target_pairs={{0,20},{16,0},{4,16},{20,4},{1,21},{17,1},{5,17},{21,5},{2,22},{18... | collective-permute-start | bytes 983048 | tf_op jit(solution)/shard_map/ppermute | solution.py:356
  382.2 30.1 %collective-permute-start.80 = (bf16[512,1280]{1,0:T(8,128)(2,1)}, bf16[512,1280]{1,0:T(8,128)(2,1)S(1)}, u32[]{:S(2)}, u32[]{:S(2)}) collective-permute-start(bf16[512,1280]{1,0:T(8,128)(2,1)} %get-tuple-element.81), channel_id=1, source_target_pairs={{0,8},{8,0},{1,9},{9,1},{2,10},{10,2},{3,11},{11,3},{4,12},{12,4},... | collective-permute-start | bytes 3932168 | tf_op jit(solution)/shard_map/ppermute | solution.py:382
  385.2 23.2 %collective-permute-start.69 = (bf16[320,640]{1,0:T(8,128)(2,1)S(1)}, bf16[320,640]{1,0:T(8,128)(2,1)S(1)}, u32[]{:S(2)}, u32[]{:S(2)}) collective-permute-start(bf16[320,640]{1,0:T(8,128)(2,1)S(1)} %copy-done.40), channel_id=1, source_target_pairs={{0,64},{32,96},{64,0},{96,32},{1,65},{33,97},{65,1},{97,33},{2,66}... | collective-permute-start | bytes 1228808 | tf_op jit(solution)/shard_map/ppermute | solution.py:351
  420.9 20.9 %all-to-all-start.1 = ((bf16[8,10,1152]{2,1,0:T(8,128)(2,1)}), bf16[8,10,1152]{2,1,0:T(8,128)(2,1)}, u32[]{:S(2)}, u32[]{:S(2)}) async-start(bf16[8,10,1152]{2,1,0:T(8,128)(2,1)} %reshape.93), calls=%async_computation.1 | async-start | bytes 589824 | tf_op jit(solution)/shard_map/all_to_all | solution.py:581
  (152 other events, 1926.5 us)
